TPU v7x, 128 devices: a whole 4x4x4 slice. The times are simulated.
128 devices in a mesh: group: 2 (over y_hi), tile: 64 (over x, y_lo, z, core).
Axes of the slice: x: 4, y: 4 (y_hi: 2, y_lo: 2; y = y_hi * 2 + y_lo), z: 4, core: 2. Of those that a mesh axis runs over, the one named last changes fastest.
Arguments:
- pressure: float32 [60, 1536, 384], P(None, ('group', 'tile')), may hold values from -6 to 6
- wind_x: float32 [60, 1536, 384], P(None, ('group', 'tile')), may hold values from -6 to 6
- wind_y: float32 [60, 1536, 384], P(None, ('group', 'tile')), may hold values from -6 to 6
- courant: float32 [60], replicated, may hold values from 0.2 to 0.6
- send_list: int32 [128, 128, 36], P(('group', 'tile')), may hold values from -1 to 4607, as said below
- norm_gain: float32 [180], replicated, may hold values from 0.25 to 1.75
- w_first: bfloat16 [180, 1024], replicated, may hold values from -0.4375 to 0.4375
- b_first: float32 [1024], replicated, may hold values from -3 to 3
- w_second: bfloat16 [1024, 1024], replicated, may hold values from -0.1875 to 0.1875
- b_second: float32 [1024], replicated, may hold values from -3 to 3
- w_last: bfloat16 [1024, 180], replicated, may hold values from -0.1875 to 0.1875
Outputs:
- new_pressure: float32 [60, 1536, 384], P(None, ('group', 'tile'))
- new_wind_x: float32 [60, 1536, 384], P(None, ('group', 'tile'))
- new_wind_y: float32 [60, 1536, 384], P(None, ('group', 'tile'))
Inputs may be any that keep to these rules, and one draw needn't show every extreme that they name: For each device d there is a count v_d: in every send_list[d, j] the first v_d entries are local columns of d and the rest are -1; no column is listed twice. In each aligned four of devices one has v_d = 36 and the four counts add up to 48, so each physics shard treats 1536 columns.
All inputs are finite; a program needn't handle non-finite values.
Results may differ from a plain program's by a relative error of at most 0.0015.
Values may be sent and summed in bfloat16 or wider, within the bound.
No kernel may reach another device: no remote copies, remote signals or barrier semaphores. Data moves between devices by JAX's collectives and lax.ppermute only.
A program may use at most 128 MiB of HBM per device.

v0:
```python
import jax
import jax.numpy as jnp
from jax import lax
from jax.experimental import pallas as pl
from jax.experimental.pallas import tpu as pltpu
from jax.sharding import PartitionSpec as P

AXES = ("group", "tile")
LEVELS, WIDTH, ACROSS, UNITS, SLOTS, DEVICES = 60, 12, 384, 1024, 36, 128
ROWS = 3 * LEVELS
HALO = 6
SPAN = WIDTH + 2 * HALO
CHUNK = 2 * ACROSS
TILE = 256
F32, BF16 = jnp.float32, jnp.bfloat16
NN = (((1,), (0,)), ((), ()))
NT = (((1,), (1,)), ((), ()))
ANY = pl.BlockSpec(memory_space=pl.ANY)
VMEM = pl.BlockSpec(memory_space=pltpu.VMEM)


def lanes(shape):
    return lax.broadcasted_iota(jnp.int32, shape, len(shape) - 1)


def run_copies(pairs, sems, first=0):
    copies = [
        pltpu.make_async_copy(src, dst, sems.at[first + i]) for i, (src, dst) in enumerate(pairs)
    ]
    for copy in copies:
        copy.start()
    return copies


def edges_kernel(p_hbm, u_hbm, v_hbm, to_next, to_prev, u_mem, v_mem, r_mem, l_mem, sems):
    loads = run_copies([(u_hbm, u_mem), (v_hbm, v_mem)], sems)
    plain = run_copies(
        [
            (p_hbm.at[WIDTH - HALO :], to_next.at[:HALO]),
            (p_hbm.at[:HALO], to_prev.at[:HALO]),
        ],
        sems,
        2,
    )
    for copy in loads:
        copy.wait()

    def divergence(x):
        v = v_mem[x]
        v = jnp.where(lanes(v.shape) < ACROSS - 1, v, 0.0)
        return v - pltpu.roll(v, 1, 1)

    total = jnp.zeros((LEVELS, ACROSS), F32)
    for i in range(HALO):
        x = WIDTH - 1 - i
        r_mem[HALO - 1 - i] = u_mem[x] - total
        if i < HALO - 1:
            total = total + divergence(x)
    total = jnp.zeros((LEVELS, ACROSS), F32)
    for x in range(HALO):
        total = total + divergence(x)
        l_mem[x] = u_mem[x] + total
    stores = run_copies(
        [(r_mem, to_next.at[HALO:]), (l_mem, to_prev.at[HALO:])],
        sems,
        4,
    )
    for copy in plain + stores:
        copy.wait()


def edges(p, u, v):
    shape = jax.ShapeDtypeStruct((2 * HALO, LEVELS, ACROSS), F32)
    return pl.pallas_call(
        edges_kernel,
        out_shape=(shape, shape),
        in_specs=[ANY] * 3,
        out_specs=(ANY, ANY),
        scratch_shapes=[
            pltpu.VMEM((WIDTH, LEVELS, ACROSS), F32),
            pltpu.VMEM((WIDTH, LEVELS, ACROSS), F32),
            pltpu.VMEM((HALO, LEVELS, ACROSS), F32),
            pltpu.VMEM((HALO, LEVELS, ACROSS), F32),
            pltpu.SemaphoreType.DMA((6,)),
        ],
        name="edges",
    )(p, u, v)


def march(count, low, high, square, load_p, load_u, load_v, done):
    ps = [{} for _ in range(count + 1)]
    us = [{} for _ in range(count + 1)]
    vs = [{} for _ in range(count + 1)]

    def advance(k, x):
        here, east = ps[k - 1][x], ps[k - 1][x + 1]
        us[k][x] = us[k - 1][x] - (east - here)
        if x < low + k:
            if k == count:
                done(x, None, us[k][x], None)
            return
        north = pltpu.roll(here, ACROSS - 1, 1)
        v = vs[k - 1][x]
        v = here - north if v is None else v - (north - here)
        v = jnp.where(lanes(v.shape) < ACROSS - 1, v, 0.0)
        vs[k][x] = v
        flow = (us[k][x] - us[k][x - 1]) + (v - pltpu.roll(v, 1, 1))
        ps[k][x] = here - square * flow
        if k == count:
            done(x, ps[k][x], us[k][x], v)
        elif x - 1 >= low + k:
            advance(k + 1, x - 1)

    ps[0][low] = load_p(low)
    for x in range(low, high):
        ps[0][x + 1] = load_p(x + 1)
        us[0][x] = load_u(x)
        if x > low:
            vs[0][x] = load_v(x)
        advance(1, x)


def by_level(row):
    return jnp.broadcast_to(row, (128, row.shape[1])).T


def by_groups(work):
    def group(g, carry):
        work(pl.ds(pl.multiple_of(g * 8, 8), 8))
        return carry

    lax.fori_loop(0, LEVELS // 8, group, 0)
    work(slice(LEVELS // 8 * 8, LEVELS))


def level_constants(courant_row, c_mem):
    c = by_level(courant_row)
    c_mem[0] = c
    c_mem[1] = c * c
    c_mem[2] = 1.0 / c


def group_constants(c_mem, rows):
    wide = lambda i: jnp.concatenate([c_mem[i, rows, :]] * 3, axis=1)
    return wide(0), wide(1), wide(2)


def silu(z):
    half = z * 0.5
    return half + half * jnp.tanh(half)


def normed_columns(state, gain, xs):
    columns = jnp.concatenate(
        [jnp.concatenate([f[x] for f in state], axis=0) for x in xs], axis=1
    )
    values = columns.astype(BF16).astype(F32)
    mean = jnp.sum(values * values, axis=0, keepdims=True) * (1.0 / ROWS)
    return (values * lax.rsqrt(mean + 1e-05) * gain).astype(BF16)


def network(normed, w1, b1, w2, b2, w3, h1, h2):
    rows = normed.T
    for n in range(0, UNITS, TILE):
        z = lax.dot_general(rows, w1[:, n : n + TILE], NN, preferred_element_type=F32)
        h1[:, n : n + TILE] = silu(z + b1[:, n : n + TILE]).astype(BF16)
    for n in range(0, UNITS, TILE):
        z = lax.dot_general(h1[...], w2[:, n : n + TILE], NN, preferred_element_type=F32)
        h2[:, n : n + TILE] = silu(z + b2[:, n : n + TILE]).astype(BF16)
    t = lax.dot_general(h2[...], w3[...], NN, preferred_element_type=F32)
    return t.T.astype(BF16).astype(F32)


def keep_listed(t, mask, x):
    row = jnp.concatenate([mask[3 * x + j : 3 * x + j + 1, :] for j in range(3)], axis=1)
    return jnp.where(row > 0.5, t, 0.0)


def store_tendency(t, mask, xs, places, out):
    for i, (x, place) in enumerate(zip(xs, places)):
        listed = keep_listed(t[:, i * ACROSS : (i + 1) * ACROSS], mask, x)
        for f in range(3):
            out[place, f] = listed[f * LEVELS : (f + 1) * LEVELS]


WEIGHTS_SCRATCH = [
    pltpu.VMEM((ROWS, UNITS), BF16),
    pltpu.VMEM((1, UNITS), F32),
    pltpu.VMEM((UNITS, UNITS), BF16),
    pltpu.VMEM((1, UNITS), F32),
    pltpu.VMEM((ROWS, UNITS), BF16),
    pltpu.VMEM((UNITS, ROWS), BF16),
    pltpu.VMEM((CHUNK, UNITS), BF16),
    pltpu.VMEM((CHUNK, UNITS), BF16),
]


def network_flops(columns):
    return 2 * columns * (2 * ROWS * UNITS + UNITS * UNITS)


def interior_kernel(
    p_hbm, u_hbm, v_hbm, w1_hbm, b1_hbm, w2_hbm, b2_hbm, w3_hbm, courant, gain, lists,
    tend, mask,
    p_mem, u_mem, v_mem, a_mem, b_mem, d_mem, c_mem, one_x, one_y,
    w1, b1, w2, b2, w3t, w3, h1, h2, sems,
):
    fields = run_copies([(p_hbm, p_mem), (u_hbm, u_mem),
                         (v_hbm, v_mem)], sems)
    weights = run_copies([(w1_hbm, w1), (b1_hbm, b1), (w2_hbm, w2), (b2_hbm, b2),
                          (w3_hbm, w3t)], sems, 3)
    level_constants(courant[...], c_mem)
    gain_column = by_level(gain[...])[:, :1]
    for s in range(SLOTS):
        entry = lists[s]
        part, spot = entry >> 7, entry & 127
        where = slice(s * DEVICES, (s + 1) * DEVICES)
        one_x[:, where] = (
            lax.broadcasted_iota(jnp.int32, (48, DEVICES), 0) == part
        ).astype(F32).astype(BF16)
        one_y[:, where] = (
            lax.broadcasted_iota(jnp.int32, (128, DEVICES), 0) == spot
        ).astype(F32).astype(BF16)
    mask[...] = lax.dot_general(one_x[...], one_y[...], NT, preferred_element_type=F32)
    for copy in fields:
        copy.wait()

    def group(rows):
        c, square, inverse = group_constants(c_mem, rows)

        def done(x, p, u, v):
            if p is not None:
                a_mem[x - 3, rows, :] = p
                b_mem[x - 3, rows, :] = u * c
                d_mem[x - 3, rows, :] = v * c

        march(3, 0, WIDTH - 1, square,
              lambda x: p_mem[x, rows, :],
              lambda x: u_mem[x, rows, :] * inverse,
              lambda x: v_mem[x, rows, :] * inverse, done)

    by_groups(group)
    for copy in weights:
        copy.wait()
    w3[...] = w3t[...].T
    for i in range(3):
        xs = (2 * i, 2 * i + 1)
        t = network(normed_columns((a_mem, b_mem, d_mem), gain_column, xs), w1, b1, w2, b2, w3, h1, h2)
        store_tendency(t, mask, [x + 3 for x in xs], xs, tend)


def interior(p, u, v, weights, courant, gain, lists):
    column = pltpu.VMEM((WIDTH, LEVELS, ACROSS), F32)
    middle = pltpu.VMEM((WIDTH // 2, LEVELS, ACROSS), F32)
    return pl.pallas_call(
        interior_kernel,
        out_shape=(
            jax.ShapeDtypeStruct((WIDTH // 2, 3, LEVELS, ACROSS), F32),
            jax.ShapeDtypeStruct((48, 128), F32),
        ),
        in_specs=[ANY] * 8 + [VMEM] * 3,
        out_specs=(VMEM, VMEM),
        scratch_shapes=[column] * 3 + [middle] * 3
        + [pltpu.VMEM((3, LEVELS, 128), F32)]
        + [pltpu.VMEM((48, SLOTS * DEVICES), BF16), pltpu.VMEM((128, SLOTS * DEVICES), BF16)]
        + WEIGHTS_SCRATCH
        + [pltpu.SemaphoreType.DMA((8,))],
        compiler_params=pltpu.CompilerParams(vmem_limit_bytes=44 * 2**20),
        cost_estimate=pl.CostEstimate(
            flops=network_flops(WIDTH // 2 * ACROSS), bytes_accessed=8 * 2**20, transcendentals=0
        ),
        name="interior",
    )(p, u, v, *weights, courant, gain, lists)


def finish_kernel(
    p_hbm, u_hbm, v_hbm, left, right, tend, w1_hbm, b1_hbm, w2_hbm, b2_hbm, w3_hbm,
    mask, courant, gain,
    p_out, u_out, v_out,
    p_mem, u_mem, v_mem, a_mem, b_mem, d_mem, t_mem, c_mem,
    w1, b1, w2, b2, w3t, w3, h1, h2, sems,
):
    own = slice(HALO, HALO + WIDTH)
    fields = run_copies(
        [
            (p_hbm, p_mem.at[own]),
            (u_hbm, u_mem.at[own]),
            (v_hbm, v_mem.at[own]),
            (left.at[:HALO], p_mem.at[:HALO]),
            (left.at[HALO:], u_mem.at[:HALO]),
            (right.at[:HALO], p_mem.at[HALO + WIDTH :]),
            (right.at[HALO:], u_mem.at[HALO + WIDTH :]),
        ],
        sems,
    )
    weights = run_copies([(w1_hbm, w1), (b1_hbm, b1), (w2_hbm, w2), (b2_hbm, b2),
                          (w3_hbm, w3t), (tend, t_mem.at[3:9])], sems, 7)
    level_constants(courant[...], c_mem)
    gain_column = by_level(gain[...])[:, :1]
    for copy in fields:
        copy.wait()

    def first_half(rows):
        c, square, inverse = group_constants(c_mem, rows)

        def done(x, p, u, v):
            u_mem[x + HALO, rows, :] = u
            if p is None:
                return
            p_mem[x + HALO, rows, :] = p
            v_mem[x + HALO, rows, :] = v
            if 0 <= x < 3 or 9 <= x < 12:
                at = x if x < 3 else x - 6
                a_mem[at, rows, :] = p
                b_mem[at, rows, :] = u * c
                d_mem[at, rows, :] = v * c

        march(3, -HALO, WIDTH + HALO - 1, square,
              lambda x: p_mem[x + HALO, rows, :],
              lambda x: u_mem[x + HALO, rows, :] * inverse,
              lambda x: v_mem[x + HALO, rows, :] * inverse if 0 <= x < WIDTH else None, done)

    by_groups(first_half)
    for copy in weights:
        copy.wait()
    w3[...] = w3t[...].T
    columns = (0, 1, 2, 9, 10, 11)
    for i in range(3):
        places = (2 * i, 2 * i + 1)
        xs = [columns[j] for j in places]
        t = network(normed_columns((a_mem, b_mem, d_mem), gain_column, places), w1, b1, w2, b2, w3, h1, h2)
        store_tendency(t, mask, xs, xs, t_mem)

    def second_half(rows):
        c, square, inverse = group_constants(c_mem, rows)

        def done(x, p, u, v):
            if p is None:
                return
            p_mem[x, rows, :] = p + t_mem[x, 0, rows, :]
            u_mem[x, rows, :] = u * c + t_mem[x, 1, rows, :]
            v_mem[x, rows, :] = v * c + t_mem[x, 2, rows, :]

        march(3, -3, WIDTH + 2, square,
              lambda x: p_mem[x + HALO, rows, :],
              lambda x: u_mem[x + HALO, rows, :],
              lambda x: v_mem[x + HALO, rows, :], done)

    by_groups(second_half)
    outs = run_copies(
        [(m.at[:WIDTH], o) for m, o in ((p_mem, p_out), (u_mem, u_out), (v_mem, v_out))],
        sems,
    )
    for copy in outs:
        copy.wait()


def finish(p, u, v, left, right, tend, weights, mask, courant, gain):
    shape = jax.ShapeDtypeStruct((WIDTH, LEVELS, ACROSS), F32)
    span = pltpu.VMEM((SPAN, LEVELS, ACROSS), F32)
    half = pltpu.VMEM((WIDTH // 2, LEVELS, ACROSS), F32)
    return pl.pallas_call(
        finish_kernel,
        out_shape=(shape,) * 3,
        in_specs=[ANY] * 11 + [VMEM] * 3,
        out_specs=(ANY,) * 3,
        scratch_shapes=[span] * 3 + [half] * 3
        + [pltpu.VMEM((WIDTH, 3, LEVELS, ACROSS), F32), pltpu.VMEM((3, LEVELS, 128), F32)]
        + WEIGHTS_SCRATCH
        + [pltpu.SemaphoreType.DMA((13,))],
        compiler_params=pltpu.CompilerParams(vmem_limit_bytes=50 * 2**20),
        cost_estimate=pl.CostEstimate(
            flops=network_flops(WIDTH // 2 * ACROSS), bytes_accessed=12 * 2**20, transcendentals=0
        ),
        name="finish",
    )(p, u, v, left, right, tend, *weights, mask, courant, gain)


def body(
    pressure, wind_x, wind_y, courant, send_list,
    norm_gain, w_first, b_first, w_second, b_second, w_last,
):
    p, u, v = [jnp.transpose(f, (1, 0, 2)) for f in (pressure, wind_x, wind_y)]
    courant, gain = courant.reshape(1, LEVELS), norm_gain.reshape(1, ROWS)
    lists = jnp.transpose(send_list, (2, 0, 1))
    weights = (w_first, b_first.reshape(1, UNITS), w_second, b_second.reshape(1, UNITS), w_last.T)
    to_next, to_prev = edges(p, u, v)
    left = lax.ppermute(to_next, AXES, [(i, (i + 1) % DEVICES) for i in range(DEVICES)])
    right = lax.ppermute(to_prev, AXES, [(i, (i - 1) % DEVICES) for i in range(DEVICES)])
    tend, mask = interior(p, u, v, weights, courant, gain, lists)
    outs = finish(p, u, v, left, right, tend, weights, mask, courant, gain)
    return tuple(jnp.transpose(f, (1, 0, 2)) for f in outs)


def solution(mesh):
    split = P(None, AXES, None)
    in_specs = (split,) * 3 + (P(), P(AXES, None, None)) + (P(),) * 6
    return jax.shard_map(
        body, mesh=mesh, in_specs=in_specs, out_specs=(split,) * 3, check_vma=False
    )
```

profile of v0, /device:TPU:0, one launch (start us, length us, event | category | flops | bytes accessed | tf_op | source)
XLA Modules:
  0.0 91.8 jit_solution(1331124616017547901)
XLA Ops:
  0.6 0.0 copy-start
  0.6 0.0 copy-start.1
  0.7 0.0 copy-start.2
  0.7 0.0 copy-start.9
  0.7 0.0 copy-start.10
  0.7 0.0 copy-start.11
  0.7 0.0 copy-start.12
  0.7 36.9 %edges.1 = (f32[12,60,384]{2,1,0:T(8,128)}, f32[12,60,384]{2,1,0:T(8,128)}) custom-call(f32[12,60,384]{2,1,0:T(8,128)} %bitcast.12, f32[12,60,384]{2,1,0:T(8,128)} %bitcast.15, f32[12,60,384]{2,1,0:T(8,128)} %bitcast.18), custom_call_target="tpu_custom_call" | custom-call | tf_op jit(solution)/shard_map/edges/pallas_call | solution.py:74
  37.6 0.1 collective-permute-start
  37.7 8.3 %collective-permute-start.1 = (f32[12,60,384]{2,1,0:T(8,128)}, f32[12,60,384]{2,1,0:T(8,128)S(1)}, u32[]{:S(2)}, u32[]{:S(2)}) collective-permute-start(f32[12,60,384]{2,1,0:T(8,128)} %get-tuple-element.11), channel_id=1, source_target_pairs={{0,127},{1,0},{2,1},{3,2},{4,3},{5,4},{6,5},{7,6},{8,7},{9,8},{10,... | collective-permute-start | bytes 3317768 | tf_op jit(solution)/shard_map/ppermute | solution.py:389
  46.0 0.0 copy-done
  46.0 0.0 copy-done.1
  46.0 0.0 copy-done.2
  46.0 0.0 copy-done.9
  46.0 0.0 copy-done.10
  46.0 0.0 copy-done.11
  46.0 0.0 copy-done.12
  46.0 0.0 copy-start.3
  46.0 1.6 %copy-done.3 = bf16[1024,1024]{1,0:T(8,128)(2,1)S(1)} copy-done((bf16[1024,1024]{1,0:T(8,128)(2,1)S(1)}, bf16[1024,1024]{1,0:T(8,128)(2,1)}, u32[]{:S(2)}) %copy-start.3) | copy-done | bytes 2097176
  47.6 1.0 %copy-done.4 = bf16[180,1024]{1,0:T(8,128)(2,1)S(1)} copy-done((bf16[180,1024]{1,0:T(8,128)(2,1)S(1)}, bf16[180,1024]{1,0:T(8,128)(2,1)}, u32[]{:S(2)}) %copy-start.4) | copy-done | bytes 368664
  48.6 1.0 %copy-done.6 = bf16[1024,180]{0,1:T(8,128)(2,1)S(1)} copy-done((bf16[1024,180]{0,1:T(8,128)(2,1)S(1)}, bf16[1024,180]{0,1:T(8,128)(2,1)}, u32[]{:S(2)}) %copy-start.6) | copy-done | bytes 368664
  49.6 0.7 copy-done.8
  50.3 14.6 %interior.1 = (f32[6,3,60,384]{3,2,1,0:T(8,128)S(1)}, f32[48,128]{1,0:T(8,128)S(1)}) custom-call(f32[12,60,384]{2,1,0:T(8,128)S(1)} %bitcast.13, f32[12,60,384]{2,1,0:T(8,128)S(1)} %bitcast.16, f32[12,60,384]{2,1,0:T(8,128)S(1)} %bitcast.20, bf16[180,1024]{1,0:T(8,128)(2,1)S(1)} %copy-done.4, f32[1,1024]{1,0:T(1,128)S(1)} %bitcast.24, ...), custom_call_target="tpu_custom_call" | custom-call | flops 6530531328 | bytes 8388608 | tf_op jit(solution)/shard_map/interior/pallas_call | solution.py:255
  64.9 0.0 copy-start.13
  65.0 1.2 %copy-done.13 = f32[6,3,60,384]{3,2,1,0:T(8,128)} copy-done((f32[6,3,60,384]{3,2,1,0:T(8,128)}, f32[6,3,60,384]{3,2,1,0:T(8,128)S(1)}, u32[]{:S(2)}) %copy-start.13) | copy-done | bytes 1658904
  66.2 0.0 collective-permute-done.left
  66.2 0.0 collective-permute-done.1.right
  66.2 0.0 copy-start.15
  66.2 1.0 %copy-done.14 = f32[12,60,384]{2,1,0:T(8,128)} copy-done((f32[12,60,384]{2,1,0:T(8,128)}, f32[12,60,384]{2,1,0:T(8,128)S(1)}, u32[]{:S(2)}) %copy-start.14) | copy-done | bytes 1105944
  67.2 0.4 copy-done.15
  67.6 0.0 copy-done.5
  67.6 24.0 %finish.1 = (f32[12,60,384]{2,1,0:T(8,128)}, f32[12,60,384]{2,1,0:T(8,128)}, f32[12,60,384]{2,1,0:T(8,128)}) custom-call(f32[12,60,384]{2,1,0:T(8,128)S(1)} %bitcast.14, f32[12,60,384]{2,1,0:T(8,128)S(1)} %bitcast.17, f32[12,60,384]{2,1,0:T(8,128)} %bitcast.19, f32[12,60,384]{2,1,0:T(8,128)} %copy-done.14, f32[12,60,384]{2,1,0:T(8,128)} %copy-done.15, ...), custom_call_target="tpu_custom_call" | custom-call | flops 6530531328 | bytes 12582912 | tf_op jit(solution)/shard_map/finish/pallas_call | solution.py:362
  (7 shorter events, 0.0 us)
Async XLA Ops:
  0.6 45.3 %copy-start = (f32[60,12,384]{2,0,1:T(8,128)S(1)}, f32[60,12,384]{2,0,1:T(8,128)}, u32[]{:S(2)}) copy-start(f32[60,12,384]{2,0,1:T(8,128)} %param.11) | copy-start | bytes 3317764
  0.6 45.3 %copy-start.1 = (f32[60,12,384]{2,0,1:T(8,128)S(1)}, f32[60,12,384]{2,0,1:T(8,128)}, u32[]{:S(2)}) copy-start(f32[60,12,384]{2,0,1:T(8,128)} %param.12) | copy-start | bytes 3317764
  0.7 45.3 %copy-start.2 = (f32[60,12,384]{2,0,1:T(8,128)S(1)}, f32[60,12,384]{2,0,1:T(8,128)}, u32[]{:S(2)}) copy-start(f32[60,12,384]{2,0,1:T(8,128)} %param.13) | copy-start | bytes 3317764
  0.7 45.3 %copy-start.9 = (f32[1024]{0:T(1024)S(1)}, f32[1024]{0:T(1024)}, u32[]{:S(2)}) copy-start(f32[1024]{0:T(1024)} %param.18) | copy-start | bytes 12292
  0.7 45.3 %copy-start.10 = (f32[1024]{0:T(1024)S(1)}, f32[1024]{0:T(1024)}, u32[]{:S(2)}) copy-start(f32[1024]{0:T(1024)} %param.20) | copy-start | bytes 12292
  0.7 45.3 %copy-start.11 = (f32[180]{0:T(256)S(1)}, f32[180]{0:T(256)}, u32[]{:S(2)}) copy-start(f32[180]{0:T(256)} %param.16) | copy-start | bytes 2164
  0.7 45.3 %copy-start.12 = (f32[60]{0:T(128)S(1)}, f32[60]{0:T(128)}, u32[]{:S(2)}) copy-start(f32[60]{0:T(128)} %param.14) | copy-start | bytes 724
  37.6 28.6 %collective-permute-start = (f32[12,60,384]{2,1,0:T(8,128)}, f32[12,60,384]{2,1,0:T(8,128)S(1)}, u32[]{:S(2)}, u32[]{:S(2)}) collective-permute-start(f32[12,60,384]{2,1,0:T(8,128)} %get-tuple-element.10), channel_id=1, source_target_pairs={{0,1},{1,2},{2,3},{3,4},{4,5},{5,6},{6,7},{7,8},{8,9},{9,10},{10,1... | collective-permute-start | bytes 3317768 | tf_op jit(solution)/shard_map/ppermute | solution.py:388
  37.7 28.5 %collective-permute-start.1 = (f32[12,60,384]{2,1,0:T(8,128)}, f32[12,60,384]{2,1,0:T(8,128)S(1)}, u32[]{:S(2)}, u32[]{:S(2)}) collective-permute-start(f32[12,60,384]{2,1,0:T(8,128)} %get-tuple-element.11), channel_id=1, source_target_pairs={{0,127},{1,0},{2,1},{3,2},{4,3},{5,4},{6,5},{7,6},{8,7},{9,8},{10,... | collective-permute-start | bytes 3317768 | tf_op jit(solution)/shard_map/ppermute | solution.py:389
  46.0 1.6 %copy-start.3 = (bf16[1024,1024]{1,0:T(8,128)(2,1)S(1)}, bf16[1024,1024]{1,0:T(8,128)(2,1)}, u32[]{:S(2)}) copy-start(bf16[1024,1024]{1,0:T(8,128)(2,1)} %w2_hbm.3) | copy-start | bytes 6291460
  47.6 1.0 %copy-start.4 = (bf16[180,1024]{1,0:T(8,128)(2,1)S(1)}, bf16[180,1024]{1,0:T(8,128)(2,1)}, u32[]{:S(2)}) copy-start(bf16[180,1024]{1,0:T(8,128)(2,1)} %w1_hbm.3) | copy-start | bytes 1105924
  48.6 1.0 %copy-start.6 = (bf16[1024,180]{0,1:T(8,128)(2,1)S(1)}, bf16[1024,180]{0,1:T(8,128)(2,1)}, u32[]{:S(2)}) copy-start(bf16[1024,180]{0,1:T(8,128)(2,1)} %param.21) | copy-start | bytes 1105924
  49.6 0.7 copy-start.8
  50.3 17.3 %copy-start.5 = (bf16[180,1024]{1,0:T(8,128)(2,1)S(1)}, bf16[180,1024]{1,0:T(8,128)(2,1)}, u32[]{:S(2)}) copy-start(bf16[180,1024]{1,0:T(8,128)(2,1)} %w1_hbm.3) | copy-start | bytes 1105924
  50.3 17.3 %copy-start.7 = (bf16[1024,180]{0,1:T(8,128)(2,1)S(1)}, bf16[1024,180]{0,1:T(8,128)(2,1)}, u32[]{:S(2)}) copy-start(bf16[1024,180]{0,1:T(8,128)(2,1)} %param.21) | copy-start | bytes 1105924
  64.9 1.2 %copy-start.13 = (f32[6,3,60,384]{3,2,1,0:T(8,128)}, f32[6,3,60,384]{3,2,1,0:T(8,128)S(1)}, u32[]{:S(2)}) copy-start(f32[6,3,60,384]{3,2,1,0:T(8,128)S(1)} %get-tuple-element.12.tend) | copy-start | bytes 4976644
  66.2 1.0 %copy-start.14 = (f32[12,60,384]{2,1,0:T(8,128)}, f32[12,60,384]{2,1,0:T(8,128)S(1)}, u32[]{:S(2)}) copy-start(f32[12,60,384]{2,1,0:T(8,128)S(1)} %collective-permute-done.left) | copy-start | bytes 3317764
  66.2 1.4 %copy-start.15 = (f32[12,60,384]{2,1,0:T(8,128)}, f32[12,60,384]{2,1,0:T(8,128)S(1)}, u32[]{:S(2)}) copy-start(f32[12,60,384]{2,1,0:T(8,128)S(1)} %collective-permute-done.1.right) | copy-start | bytes 3317764
where the time goes:
time: 92.1 us; the launch traced here: 91.8 us
  Pallas kernels  75.5 us (82%)
  starting transfers between devices  8.35 us (9%)
  local copies, waits for them, and re-layouts  6.97 us (8%)
  between operations  0.94 us (1%)
    pallas_call x1, Pallas kernels, edges(): pl.pallas_call(edges_kernel, out_shape=(shape, shape), in_specs=[ANY] * 3...  36.9 us
    pallas_call x1, Pallas kernels, finish(): pl.pallas_call(finish_kernel, out_shape=(shape,) * 3, in_specs=[ANY] * 11...  24 us
    pallas_call x1, Pallas kernels, interior(): pl.pallas_call(interior_kernel, out_shape=(jax.ShapeDtypeStruct((WIDTH //...  14.6 us
    ppermute x1, starting transfers between devices, body(): lax.ppermute(to_prev, AXES, [(i, (i - 1) % DEVICES) for i in range(DEVICE...  8.27 us
    unnamed x32, local copies, waits for them, and re-layouts  6.97 us
  transfers between devices with their start and end apart: 2, of which 0 were waited for; matrix products, arithmetic and copies ran while one was open for 0% of the time, Pallas kernels for 16%

commit v1 on v0

v1 whole, which is shorter than its diff:
```python
import jax
import jax.numpy as jnp
from jax import lax
from jax.experimental import pallas as pl
from jax.experimental.pallas import tpu as pltpu
from jax.sharding import PartitionSpec as P

AXES = ("group", "tile")
LEVELS, WIDTH, ACROSS, UNITS, SLOTS, DEVICES = 60, 12, 384, 1024, 36, 128
ROWS = 3 * LEVELS
HALO = 6
SPAN = WIDTH + 2 * HALO
CHUNK = 2 * ACROSS
TILE = 256
F32, BF16 = jnp.float32, jnp.bfloat16
NN = (((1,), (0,)), ((), ()))
NT = (((1,), (1,)), ((), ()))
ANY = pl.BlockSpec(memory_space=pltpu.HBM)
VMEM = pl.BlockSpec(memory_space=pltpu.VMEM)


def lanes(shape):
    return lax.broadcasted_iota(jnp.int32, shape, len(shape) - 1)


def split(value):
    return [value[:, i : i + 128] for i in range(0, ACROSS, 128)]


def join(parts):
    return jnp.concatenate(parts, axis=1)


def run_copies(pairs, sems, first=0):
    copies = [
        pltpu.make_async_copy(src, dst, sems.at[first + i]) for i, (src, dst) in enumerate(pairs)
    ]
    for copy in copies:
        copy.start()
    return copies


def divergence(v):
    v = jnp.where(lanes(v.shape) < ACROSS - 1, v, 0.0)
    return v - pltpu.roll(v, 1, 1)


def edges_kernel(p_hbm, u_hbm, v_hbm, to_next, to_prev, p_mem, u_mem, v_mem, r_mem, l_mem, sems):
    low, high = slice(0, HALO), slice(WIDTH - HALO, WIDTH)
    loads = run_copies(
        [(f.at[s], m.at[s]) for s in (high, low)
         for f, m in ((p_hbm, p_mem), (u_hbm, u_mem), (v_hbm, v_mem))],
        sems,
    )
    for copy in loads[:3]:
        copy.wait()
    for i in range(HALO):
        r_mem[i] = p_mem[WIDTH - HALO + i].astype(BF16)
    for i in range(HALO - 1):
        x = WIDTH - HALO + 1 + i
        r_mem[HALO + i] = ((u_mem[x] - u_mem[x - 1]) + divergence(v_mem[x])).astype(BF16)
    r_mem[2 * HALO - 1] = u_mem[WIDTH - 1].astype(BF16)
    out_next = run_copies([(r_mem, to_next)], sems, 6)
    for copy in loads[3:]:
        copy.wait()
    for i in range(HALO):
        l_mem[i] = p_mem[i].astype(BF16)
    for x in range(HALO):
        west = u_mem[x - 1] if x else 0.0
        l_mem[HALO + x] = ((u_mem[x] - west) + divergence(v_mem[x])).astype(BF16)
    for copy in out_next + run_copies([(l_mem, to_prev)], sems, 7):
        copy.wait()


def edges(p, u, v):
    shape = jax.ShapeDtypeStruct((2 * HALO, LEVELS, ACROSS), BF16)
    return pl.pallas_call(
        edges_kernel,
        out_shape=(shape, shape),
        in_specs=[ANY] * 3,
        out_specs=(ANY, ANY),
        scratch_shapes=[pltpu.VMEM((WIDTH, LEVELS, ACROSS), F32)] * 3
        + [pltpu.VMEM((2 * HALO, LEVELS, ACROSS), BF16)] * 2
        + [pltpu.SemaphoreType.DMA((8,))],
        compiler_params=pltpu.CompilerParams(vmem_limit_bytes=60 * 2**20),
        name="edges",
    )(p, u, v)


def march(count, low, high, square, load_p, load_d, done):
    ps = [{} for _ in range(count + 1)]
    ds = [{} for _ in range(count + 1)]
    sums = {}
    lane = lanes(square.shape)
    first, last = lane == 0, lane == 127

    def substep(k, x):
        west, here, east = (ps[k - 1][x + i] for i in (-1, 0, 1))
        down = [pltpu.roll(h, 127, 1) for h in here]
        up = [pltpu.roll(h, 1, 1) for h in here]
        north = [jnp.where(last, down[1], down[0]), jnp.where(last, down[2], down[1]),
                 jnp.where(last, here[2], down[2])]
        south = [jnp.where(first, here[0], up[0]), jnp.where(first, up[0], up[1]),
                 jnp.where(first, up[1], up[2])]
        ds[k][x] = [d - (((e + w) + (n + s)) - 4.0 * h)
                    for d, e, w, n, s, h in zip(ds[k - 1][x], east, west, north, south, here)]
        ps[k][x] = [h - square * d for h, d in zip(here, ds[k][x])]
        if k == count:
            done(x, ps[k][x], sums[x], sums[x + 1])
        elif low + count - 1 <= x <= high - count + 1:
            sums[x] = [s + p for s, p in zip(sums[x], ps[k][x])]

    for t in range(low, high + 2 * count + 1):
        if t <= high:
            ps[0][t] = load_p(t)
            if low + count - 1 <= t <= high - count + 1:
                sums[t] = ps[0][t]
            if low < t < high:
                ds[0][t] = load_d(t)
        for k in range(1, count + 1):
            x = t - 2 * k
            if low + k <= x <= high - k:
                substep(k, x)


def own_divergence(u, west, v, inverse):
    lane = lanes(inverse.shape)
    first, last = lane == 0, lane == 127
    v = [v[0], v[1], jnp.where(last, 0.0, v[2])]
    up = [pltpu.roll(a, 1, 1) for a in v]
    south = [jnp.where(first, up[i - 1], up[i]) for i in range(3)]
    return [((a - w) + (b - s)) * inverse for a, w, b, s in zip(u, west, v, south)]


def winds(u, v, c, here, east):
    last = lanes(c.shape) == 127
    down = [pltpu.roll(s, 127, 1) for s in here]
    north = [jnp.where(last, down[1], down[0]), jnp.where(last, down[2], down[1]), down[2]]
    u = [a - c * (e - s) for a, e, s in zip(u, east, here)]
    v = [a - c * (n - s) for a, n, s in zip(v, north, here)]
    return u, [v[0], v[1], jnp.where(last, 0.0, v[2])]


def by_level(row):
    return jnp.broadcast_to(row, (128, row.shape[1])).T


def level_constants(courant_row, c_mem):
    c = by_level(courant_row)
    c_mem[0] = c
    c_mem[1] = c * c
    c_mem[2] = 1.0 / c


def by_groups(work):
    def group(g, carry):
        work(pl.ds(pl.multiple_of(g * 8, 8), 8))
        return carry

    lax.fori_loop(0, LEVELS // 8, group, 0)
    work(slice(LEVELS // 8 * 8, LEVELS))


def silu(z):
    half = z * 0.5
    return half + half * jnp.tanh(half)


def normed_columns(state, gain, xs):
    columns = jnp.concatenate(
        [jnp.concatenate([f[x] for f in state], axis=0) for x in xs], axis=1
    )
    values = columns.astype(BF16).astype(F32)
    mean = jnp.sum(values * values, axis=0, keepdims=True) * (1.0 / ROWS)
    return (values * lax.rsqrt(mean + 1e-05) * gain).astype(BF16)


def network(normed, w1, b1, w2, b2, w3, h1, h2, beside=()):
    rows = normed.T
    for n in range(0, UNITS, TILE):
        z = lax.dot_general(rows, w1[:, n : n + TILE], NN, preferred_element_type=F32)
        h1[:, n : n + TILE] = silu(z + b1[:, n : n + TILE]).astype(BF16)
    for n in range(0, UNITS, TILE):
        z = lax.dot_general(h1[...], w2[:, n : n + TILE], NN, preferred_element_type=F32)
        h2[:, n : n + TILE] = silu(z + b2[:, n : n + TILE]).astype(BF16)
        if n // TILE < len(beside):
            beside[n // TILE]()
    t = lax.dot_general(h2[...], w3[...], NN, preferred_element_type=F32)
    return t.T.astype(BF16).astype(F32)


def keep_listed(t, mask, x):
    row = jnp.concatenate([mask[3 * x + j : 3 * x + j + 1, :] for j in range(3)], axis=1)
    return jnp.where(row > 0.5, t, 0.0)


def store_tendency(t, mask, xs, places, out):
    for i, (x, place) in enumerate(zip(xs, places)):
        listed = keep_listed(t[:, i * ACROSS : (i + 1) * ACROSS], mask, x)
        for f in range(3):
            out[place, f] = listed[f * LEVELS : (f + 1) * LEVELS]


WEIGHTS_SCRATCH = [
    pltpu.VMEM((ROWS, UNITS), BF16),
    pltpu.VMEM((1, UNITS), F32),
    pltpu.VMEM((UNITS, UNITS), BF16),
    pltpu.VMEM((1, UNITS), F32),
    pltpu.VMEM((ROWS, UNITS), BF16),
    pltpu.VMEM((UNITS, ROWS), BF16),
    pltpu.VMEM((CHUNK, UNITS), BF16),
    pltpu.VMEM((CHUNK, UNITS), BF16),
]


def network_flops(columns):
    return 2 * columns * (2 * ROWS * UNITS + UNITS * UNITS)


def interior_kernel(
    p_hbm, u_hbm, v_hbm, w1_hbm, b1_hbm, w2_hbm, b2_hbm, w3_hbm, courant, gain, lists,
    tend, mask,
    p_mem, u_mem, v_mem, a_mem, b_mem, d_mem, t_mem, c_mem, one_x, one_y,
    w1, b1, w2, b2, w3t, w3, h1, h2, sems,
):
    fields = run_copies([(p_hbm, p_mem), (u_hbm, u_mem), (v_hbm, v_mem)], sems)
    weights = run_copies([(w1_hbm, w1), (b1_hbm, b1), (w2_hbm, w2), (b2_hbm, b2),
                          (w3_hbm, w3t)], sems, 3)
    level_constants(courant[...], c_mem)
    gain_column = by_level(gain[...])[:, :1]
    for s in range(SLOTS):
        entry = lists[s]
        part, spot = entry >> 7, entry & 127
        where = slice(s * DEVICES, (s + 1) * DEVICES)
        one_x[:, where] = (
            lax.broadcasted_iota(jnp.int32, (48, DEVICES), 0) == part
        ).astype(F32).astype(BF16)
        one_y[:, where] = (
            lax.broadcasted_iota(jnp.int32, (128, DEVICES), 0) == spot
        ).astype(F32).astype(BF16)
    mask[...] = lax.dot_general(one_x[...], one_y[...], NT, preferred_element_type=F32)
    for copy in fields:
        copy.wait()

    def group(rows):
        c, square, inverse = (c_mem[i, rows, :] for i in range(3))

        def done(x, p, here, east):
            a_mem[x - 3, rows, :] = join(p)
            u, v = winds(split(u_mem[x, rows, :]), split(v_mem[x, rows, :]), c, here, east)
            b_mem[x - 3, rows, :] = join(u)
            d_mem[x - 3, rows, :] = join(v)

        def load_d(x):
            return own_divergence(split(u_mem[x, rows, :]), split(u_mem[x - 1, rows, :]),
                                  split(v_mem[x, rows, :]), inverse)

        march(3, 0, WIDTH - 1, square, lambda x: split(p_mem[x, rows, :]), load_d, done)

    by_groups(group)
    for copy in weights:
        copy.wait()
    w3[...] = w3t[...].T
    sent = []
    for i in range(3):
        xs = (2 * i, 2 * i + 1)
        t = network(normed_columns((a_mem, b_mem, d_mem), gain_column, xs), w1, b1, w2, b2, w3, h1, h2)
        store_tendency(t, mask, [x + 3 for x in xs], xs, t_mem)
        sent += run_copies([(t_mem.at[2 * i : 2 * i + 2], tend.at[2 * i : 2 * i + 2])], sems, 8 + i)
    for copy in sent:
        copy.wait()


def interior(p, u, v, weights, courant, gain, lists):
    column = pltpu.VMEM((WIDTH, LEVELS, ACROSS), F32)
    middle = pltpu.VMEM((WIDTH // 2, LEVELS, ACROSS), F32)
    return pl.pallas_call(
        interior_kernel,
        out_shape=(
            jax.ShapeDtypeStruct((WIDTH // 2, 3, LEVELS, ACROSS), F32),
            jax.ShapeDtypeStruct((48, 128), F32),
        ),
        in_specs=[ANY] * 8 + [VMEM] * 3,
        out_specs=(ANY, VMEM),
        scratch_shapes=[column] * 3 + [middle] * 3
        + [pltpu.VMEM((WIDTH // 2, 3, LEVELS, ACROSS), F32), pltpu.VMEM((3, LEVELS, 128), F32)]
        + [pltpu.VMEM((48, SLOTS * DEVICES), BF16), pltpu.VMEM((128, SLOTS * DEVICES), BF16)]
        + WEIGHTS_SCRATCH
        + [pltpu.SemaphoreType.DMA((11,))],
        compiler_params=pltpu.CompilerParams(vmem_limit_bytes=60 * 2**20),
        cost_estimate=pl.CostEstimate(
            flops=network_flops(WIDTH // 2 * ACROSS), bytes_accessed=8 * 2**20, transcendentals=0
        ),
        name="interior",
    )(p, u, v, *weights, courant, gain, lists)


def finish_kernel(
    p_hbm, u_hbm, v_hbm, left, right, tend, w1_hbm, b1_hbm, w2_hbm, b2_hbm, w3_hbm,
    mask, courant, gain,
    p_out, u_out, v_out,
    p_mem, u_mem, v_mem, e_mem, halo, a_mem, b_mem, d_mem, t_mem, c_mem, p_new, u_new, v_new,
    w1, b1, w2, b2, w3t, w3, h1, h2, sems,
):
    near, far = slice(0, HALO), slice(HALO, WIDTH)
    fields = run_copies(
        [
            (left, halo.at[0]),
            (p_hbm.at[near], p_mem.at[HALO : 2 * HALO]),
            (u_hbm.at[near], u_mem.at[near]),
            (v_hbm.at[near], v_mem.at[near]),
            (right, halo.at[1]),
            (p_hbm.at[far], p_mem.at[2 * HALO : 3 * HALO]),
            (u_hbm.at[far], u_mem.at[far]),
            (v_hbm.at[far], v_mem.at[far]),
        ],
        sems,
    )
    weights = run_copies([(w1_hbm, w1), (b1_hbm, b1), (w2_hbm, w2), (b2_hbm, b2),
                          (w3_hbm, w3t), (tend, t_mem.at[3:9])], sems, 8)
    level_constants(courant[...], c_mem)
    gain_column = by_level(gain[...])[:, :1]

    def loads(rows, inverse):
        def load_p(x):
            return split(p_mem[x + HALO, rows, :])

        def load_d(x):
            if x < 0:
                return [d * inverse for d in split(e_mem[x + HALO - 1, rows, :])]
            if x > WIDTH:
                return [d * inverse for d in split(e_mem[x - HALO, rows, :])]
            if x == WIDTH:
                return [(d - u) * inverse for d, u in zip(split(e_mem[HALO, rows, :]),
                                                          split(u_mem[WIDTH - 1, rows, :]))]
            west = u_mem[x - 1, rows, :] if x else e_mem[HALO - 1, rows, :]
            return own_divergence(split(u_mem[x, rows, :]), split(west),
                                  split(v_mem[x, rows, :]), inverse)

        return load_p, load_d

    def strip(start, low):
        def group(rows):
            c, square, inverse = (c_mem[i, rows, :] for i in range(3))

            def done(x, p, here, east):
                at = x - low - 3 + start
                a_mem[at, rows, :] = join(p)
                u, v = winds(split(u_mem[x, rows, :]), split(v_mem[x, rows, :]), c, here, east)
                b_mem[at, rows, :] = join(u)
                d_mem[at, rows, :] = join(v)

            march(3, low, low + 8, square, *loads(rows, inverse), done)

        by_groups(group)

    for copy in fields[:4]:
        copy.wait()
    for i in range(HALO):
        p_mem[i] = halo[0, i].astype(F32)
        e_mem[i] = halo[0, HALO + i].astype(F32)
    strip(0, -3)
    for copy in fields[4:]:
        copy.wait()
    for i in range(HALO):
        p_mem[HALO + WIDTH + i] = halo[1, i].astype(F32)
        e_mem[HALO + i] = halo[1, HALO + i].astype(F32)
    strip(3, 6)

    def dynamics(rows):
        c, square, inverse = (c_mem[i, rows, :] for i in range(3))

        def done(x, p, here, east):
            p_new[x, rows, :] = join(p)
            u, v = winds(split(u_mem[x, rows, :]), split(v_mem[x, rows, :]), c, here, east)
            u_new[x, rows, :] = join(u)
            v_new[x, rows, :] = join(v)

        march(6, -HALO, WIDTH + HALO - 1, square, *loads(rows, inverse), done)

    for copy in weights:
        copy.wait()
    w3[...] = w3t[...].T
    outs = []

    def send(low, high):
        for x in range(low, high):
            for f, new in enumerate((p_new, u_new, v_new)):
                new[x] = new[x] + t_mem[x, f]
        outs.extend(run_copies(
            [(new.at[low:high], out.at[low:high])
             for new, out in ((p_new, p_out), (u_new, u_out), (v_new, v_out))],
            sems, 3 * len(outs) // 3,
        ))

    columns = (0, 1, 2, 9, 10, 11)

    def groups(low, high):
        def run():
            for g in range(low, high):
                dynamics(pl.ds(8 * g, 8) if g < LEVELS // 8 else slice(LEVELS // 8 * 8, LEVELS))
        return run

    beside = (
        [groups(0, 1), groups(1, 2), groups(2, 3)],
        [groups(3, 4), groups(4, 5), groups(5, 6)],
        [groups(6, 7), groups(7, 8), lambda: send(0, 5), lambda: send(5, 10)],
    )
    for i in range(3):
        places = (2 * i, 2 * i + 1)
        xs = [columns[j] for j in places]
        t = network(normed_columns((a_mem, b_mem, d_mem), gain_column, places),
                    w1, b1, w2, b2, w3, h1, h2, beside[i])
        store_tendency(t, mask, xs, xs, t_mem)
    send(10, 12)
    for copy in outs:
        copy.wait()


def finish(p, u, v, left, right, tend, weights, mask, courant, gain):
    shape = jax.ShapeDtypeStruct((WIDTH, LEVELS, ACROSS), F32)
    column = pltpu.VMEM((WIDTH, LEVELS, ACROSS), F32)
    half = pltpu.VMEM((WIDTH // 2, LEVELS, ACROSS), F32)
    return pl.pallas_call(
        finish_kernel,
        out_shape=(shape,) * 3,
        in_specs=[ANY] * 11 + [VMEM] * 3,
        out_specs=(ANY,) * 3,
        scratch_shapes=[pltpu.VMEM((SPAN, LEVELS, ACROSS), F32)] + [column] * 3
        + [pltpu.VMEM((2, 2 * HALO, LEVELS, ACROSS), BF16)] + [half] * 3
        + [pltpu.VMEM((WIDTH, 3, LEVELS, ACROSS), F32), pltpu.VMEM((3, LEVELS, 128), F32)]
        + [column] * 3
        + WEIGHTS_SCRATCH
        + [pltpu.SemaphoreType.DMA((14,))],
        compiler_params=pltpu.CompilerParams(vmem_limit_bytes=60 * 2**20),
        cost_estimate=pl.CostEstimate(
            flops=network_flops(WIDTH // 2 * ACROSS), bytes_accessed=12 * 2**20, transcendentals=0
        ),
        name="finish",
    )(p, u, v, left, right, tend, *weights, mask, courant, gain)


def body(
    pressure, wind_x, wind_y, courant, send_list,
    norm_gain, w_first, b_first, w_second, b_second, w_last,
):
    p, u, v = [jnp.transpose(f, (1, 0, 2)) for f in (pressure, wind_x, wind_y)]
    courant, gain = courant.reshape(1, LEVELS), norm_gain.reshape(1, ROWS)
    lists = jnp.transpose(send_list, (2, 0, 1))
    weights = (w_first, b_first.reshape(1, UNITS), w_second, b_second.reshape(1, UNITS), w_last.T)
    to_next, to_prev = edges(p, u, v)
    left = lax.ppermute(to_next, AXES, [(i, (i + 1) % DEVICES) for i in range(DEVICES)])
    right = lax.ppermute(to_prev, AXES, [(i, (i - 1) % DEVICES) for i in range(DEVICES)])
    tend, mask = interior(p, u, v, weights, courant, gain, lists)
    outs = finish(p, u, v, left, right, tend, weights, mask, courant, gain)
    return tuple(jnp.transpose(f, (1, 0, 2)) for f in outs)


def solution(mesh):
    split = P(None, AXES, None)
    in_specs = (split,) * 3 + (P(), P(AXES, None, None)) + (P(),) * 6
    return jax.shard_map(
        body, mesh=mesh, in_specs=in_specs, out_specs=(split,) * 3, check_vma=False
    )
```

time: 92.1 us -> 50 us (0.54)
  Pallas kernels: 75.5 us -> 39.6 us
  local copies, waits for them, and re-layouts: 6.97 us -> 0.98 us
    pallas_call x1, Pallas kernels: 36.9 us -> 3.08 us  [edges(): pl.pallas_call(edges_kernel, out_shape=(shape, shape), in_specs=[ANY] * 3...]
    unnamed x32 -> x4, local copies, waits for them, and re-layouts: 6.97 us -> 0.98 us
    pallas_call x1, Pallas kernels: 24 us -> 20.4 us  [finish(): pl.pallas_call(finish_kernel, out_shape=(shape,) * 3, in_specs=[ANY] * 11...]
    pallas_call x1, Pallas kernels: 14.6 us -> 16.1 us  [interior(): pl.pallas_call(interior_kernel, out_shape=(jax.ShapeDtypeStruct((WIDTH //...]
  transfers between devices with their start and end apart: 2 -> 2, of which waited for: 0 -> 0; matrix products, arithmetic and copies ran while one was open for 0% -> 0% of each run, Pallas kernels for 16% -> 32%
where the time goes in v1:
time: 50 us; the launch traced here: 49.8 us
  Pallas kernels  39.6 us (79%)
  starting transfers between devices  8.35 us (17%)
  local copies, waits for them, and re-layouts  0.98 us (2%)
  between operations  0.85 us (2%)
    pallas_call x1, Pallas kernels, finish(): pl.pallas_call(finish_kernel, out_shape=(shape,) * 3, in_specs=[ANY] * 11...  20.4 us
    pallas_call x1, Pallas kernels, interior(): pl.pallas_call(interior_kernel, out_shape=(jax.ShapeDtypeStruct((WIDTH //...  16.1 us
    ppermute x1, starting transfers between devices, body(): lax.ppermute(to_prev, AXES, [(i, (i - 1) % DEVICES) for i in range(DEVICE...  8.27 us
    pallas_call x1, Pallas kernels, edges(): pl.pallas_call(edges_kernel, out_shape=(shape, shape), in_specs=[ANY] * 3...  3.08 us
  transfers between devices with their start and end apart: 2, of which 0 were waited for; matrix products, arithmetic and copies ran while one was open for 0% of the time, Pallas kernels for 32%

profile of v1, /device:TPU:0, one launch (start us, length us, event | category | flops | bytes accessed | tf_op | source)
XLA Modules:
  0.0 49.8 jit_solution(17267346133074158827)
XLA Ops:
  0.6 3.1 %edges.1 = (bf16[12,60,384]{2,1,0:T(8,128)(2,1)}, bf16[12,60,384]{2,1,0:T(8,128)(2,1)}) custom-call(f32[12,60,384]{2,1,0:T(8,128)} %bitcast.12, f32[12,60,384]{2,1,0:T(8,128)} %bitcast.15, f32[12,60,384]{2,1,0:T(8,128)} %bitcast.18), custom_call_target="tpu_custom_call" | custom-call | tf_op jit(solution)/shard_map/edges/pallas_call | solution.py:77
  3.7 0.1 collective-permute-start
  3.8 8.3 %collective-permute-start.1 = (bf16[12,60,384]{2,1,0:T(8,128)(2,1)}, bf16[12,60,384]{2,1,0:T(8,128)(2,1)S(1)}, u32[]{:S(2)}, u32[]{:S(2)}) collective-permute-start(bf16[12,60,384]{2,1,0:T(8,128)(2,1)} %get-tuple-element.11), channel_id=1, source_target_pairs={{0,127},{1,0},{2,1},{3,2},{4,3},{5,4},{6,5},{7,6},{8,7},{9,8},{10,... | collective-permute-start | bytes 1658888 | tf_op jit(solution)/shard_map/ppermute | solution.py:453
  12.1 16.1 %interior.1 = (f32[6,3,60,384]{3,2,1,0:T(8,128)}, f32[48,128]{1,0:T(8,128)}) custom-call(f32[12,60,384]{2,1,0:T(8,128)} %bitcast.13, f32[12,60,384]{2,1,0:T(8,128)} %bitcast.16, f32[12,60,384]{2,1,0:T(8,128)} %bitcast.19, bf16[180,1024]{1,0:T(8,128)(2,1)} %w1_hbm.3, f32[1,1024]{1,0:T(1,128)} %bitcast.24, bf16[1024,1024]{1,0:T(8,128)(2,1)} %w2_hbm.3, ...), custom_call_target="tpu_custom_call" | custom-call | flops 6530531328 | bytes 8388608 | tf_op jit(solution)/shard_map/interior/pallas_call | solution.py:277
  28.2 0.0 collective-permute-done.left
  28.2 0.0 copy-start
  28.2 0.0 collective-permute-done.1.right
  28.2 0.0 copy-start.1
  28.2 0.8 %copy-done = bf16[12,60,384]{2,1,0:T(8,128)(2,1)} copy-done((bf16[12,60,384]{2,1,0:T(8,128)(2,1)}, bf16[12,60,384]{2,1,0:T(8,128)(2,1)S(1)}, u32[]{:S(2)}) %copy-start) | copy-done | bytes 552984
  29.1 0.2 copy-done.1
  29.2 20.4 %finish.1 = (f32[12,60,384]{2,1,0:T(8,128)}, f32[12,60,384]{2,1,0:T(8,128)}, f32[12,60,384]{2,1,0:T(8,128)}) custom-call(f32[12,60,384]{2,1,0:T(8,128)} %bitcast.14, f32[12,60,384]{2,1,0:T(8,128)} %bitcast.17, f32[12,60,384]{2,1,0:T(8,128)} %bitcast.20, bf16[12,60,384]{2,1,0:T(8,128)(2,1)} %copy-done, bf16[12,60,384]{2,1,0:T(8,128)(2,1)} %copy-done.1, ...), custom_call_target="tpu_custom_call" | custom-call | flops 6530531328 | bytes 12582912 | tf_op jit(solution)/shard_map/finish/pallas_call | solution.py:424
Async XLA Ops:
  3.7 24.5 %collective-permute-start = (bf16[12,60,384]{2,1,0:T(8,128)(2,1)}, bf16[12,60,384]{2,1,0:T(8,128)(2,1)S(1)}, u32[]{:S(2)}, u32[]{:S(2)}) collective-permute-start(bf16[12,60,384]{2,1,0:T(8,128)(2,1)} %get-tuple-element.10), channel_id=1, source_target_pairs={{0,1},{1,2},{2,3},{3,4},{4,5},{5,6},{6,7},{7,8},{8,9},{9,10},{10,1... | collective-permute-start | bytes 1658888 | tf_op jit(solution)/shard_map/ppermute | solution.py:452
  3.8 24.4 %collective-permute-start.1 = (bf16[12,60,384]{2,1,0:T(8,128)(2,1)}, bf16[12,60,384]{2,1,0:T(8,128)(2,1)S(1)}, u32[]{:S(2)}, u32[]{:S(2)}) collective-permute-start(bf16[12,60,384]{2,1,0:T(8,128)(2,1)} %get-tuple-element.11), channel_id=1, source_target_pairs={{0,127},{1,0},{2,1},{3,2},{4,3},{5,4},{6,5},{7,6},{8,7},{9,8},{10,... | collective-permute-start | bytes 1658888 | tf_op jit(solution)/shard_map/ppermute | solution.py:453
  28.2 0.8 %copy-start = (bf16[12,60,384]{2,1,0:T(8,128)(2,1)}, bf16[12,60,384]{2,1,0:T(8,128)(2,1)S(1)}, u32[]{:S(2)}) copy-start(bf16[12,60,384]{2,1,0:T(8,128)(2,1)S(1)} %collective-permute-done.left) | copy-start | bytes 1658884
  28.2 1.0 %copy-start.1 = (bf16[12,60,384]{2,1,0:T(8,128)(2,1)}, bf16[12,60,384]{2,1,0:T(8,128)(2,1)S(1)}, u32[]{:S(2)}) copy-start(bf16[12,60,384]{2,1,0:T(8,128)(2,1)S(1)} %collective-permute-done.1.right) | copy-start | bytes 1658884

commit v2 on v1

v2 whole, which is shorter than its diff:
```python
import jax
import jax.numpy as jnp
from jax import lax
from jax.experimental import pallas as pl
from jax.experimental.pallas import tpu as pltpu
from jax.sharding import PartitionSpec as P

AXES = ("group", "tile")
LEVELS, WIDTH, ACROSS, UNITS, SLOTS, DEVICES = 60, 12, 384, 1024, 36, 128
ROWS = 3 * LEVELS
HALO = 6
SENT = 2 * HALO + 4
OPEN = pl.BlockSpec(memory_space=pl.ANY)
SPAN = WIDTH + 2 * HALO
CHUNK = 2 * ACROSS
TILE = 256
F32, BF16 = jnp.float32, jnp.bfloat16
NN = (((1,), (0,)), ((), ()))
NT = (((1,), (1,)), ((), ()))
ANY = pl.BlockSpec(memory_space=pltpu.HBM)
VMEM = pl.BlockSpec(memory_space=pltpu.VMEM)


def lanes(shape):
    return lax.broadcasted_iota(jnp.int32, shape, len(shape) - 1)


def split(value):
    return [value[:, i : i + 128] for i in range(0, ACROSS, 128)]


def join(parts):
    return jnp.concatenate(parts, axis=1)


def run_copies(pairs, sems, first=0):
    copies = [
        pltpu.make_async_copy(src, dst, sems.at[first + i]) for i, (src, dst) in enumerate(pairs)
    ]
    for copy in copies:
        copy.start()
    return copies


def divergence(v):
    v = jnp.where(lanes(v.shape) < ACROSS - 1, v, 0.0)
    return v - pltpu.roll(v, 1, 1)


def rest(value):
    return (value - value.astype(BF16).astype(F32)).astype(BF16)


def edges_kernel(p_hbm, u_hbm, v_hbm, to_next, to_prev, p_mem, u_mem, v_mem, r_mem, l_mem, sems):
    low, high = slice(0, HALO), slice(WIDTH - HALO, WIDTH)
    loads = run_copies(
        [(f.at[s], m.at[s]) for s in (high, low)
         for f, m in ((p_hbm, p_mem), (u_hbm, u_mem), (v_hbm, v_mem))],
        sems,
    )
    for copy in loads[:3]:
        copy.wait()
    for i in range(HALO):
        r_mem[i] = p_mem[WIDTH - HALO + i].astype(BF16)
    for i in range(HALO - 1):
        x = WIDTH - HALO + 1 + i
        div = (u_mem[x] - u_mem[x - 1]) + divergence(v_mem[x])
        r_mem[HALO + i] = div.astype(BF16)
        if x == WIDTH - 1:
            r_mem[2 * HALO + 2] = rest(div)
    r_mem[2 * HALO - 1] = u_mem[WIDTH - 1].astype(BF16)
    r_mem[2 * HALO] = rest(p_mem[WIDTH - 1])
    r_mem[2 * HALO + 1] = rest(p_mem[WIDTH - 2])
    r_mem[2 * HALO + 3] = rest(u_mem[WIDTH - 1])
    out_next = run_copies([(r_mem, to_next)], sems, 6)
    for copy in loads[3:]:
        copy.wait()
    for i in range(HALO):
        l_mem[i] = p_mem[i].astype(BF16)
    for x in range(HALO):
        west = u_mem[x - 1] if x else 0.0
        div = (u_mem[x] - west) + divergence(v_mem[x])
        l_mem[HALO + x] = div.astype(BF16)
        if x < 2:
            l_mem[2 * HALO + 2 + x] = rest(div)
    l_mem[2 * HALO] = rest(p_mem[0])
    l_mem[2 * HALO + 1] = rest(p_mem[1])
    for copy in out_next + run_copies([(l_mem, to_prev)], sems, 7):
        copy.wait()


def edges(p, u, v):
    shape = jax.ShapeDtypeStruct((SENT, LEVELS, ACROSS), BF16)
    return pl.pallas_call(
        edges_kernel,
        out_shape=(shape, shape),
        in_specs=[ANY] * 3,
        out_specs=(OPEN, OPEN),
        scratch_shapes=[pltpu.VMEM((WIDTH, LEVELS, ACROSS), F32)] * 3
        + [pltpu.VMEM((SENT, LEVELS, ACROSS), BF16)] * 2
        + [pltpu.SemaphoreType.DMA((8,))],
        compiler_params=pltpu.CompilerParams(vmem_limit_bytes=24 * 2**20),
        name="edges",
    )(p, u, v)


def march(count, low, high, square, load_p, load_d, done):
    ps = [{} for _ in range(count + 1)]
    ds = [{} for _ in range(count + 1)]
    sums = {}
    lane = lanes(square.shape)
    first, last = lane == 0, lane == 127

    def substep(k, x):
        west, here, east = (ps[k - 1][x + i] for i in (-1, 0, 1))
        down = [pltpu.roll(h, 127, 1) for h in here]
        up = [pltpu.roll(h, 1, 1) for h in here]
        north = [jnp.where(last, down[1], down[0]), jnp.where(last, down[2], down[1]),
                 jnp.where(last, here[2], down[2])]
        south = [jnp.where(first, here[0], up[0]), jnp.where(first, up[0], up[1]),
                 jnp.where(first, up[1], up[2])]
        ds[k][x] = [d - (((e + w) + (n + s)) - 4.0 * h)
                    for d, e, w, n, s, h in zip(ds[k - 1][x], east, west, north, south, here)]
        ps[k][x] = [h - square * d for h, d in zip(here, ds[k][x])]
        if k == count:
            done(x, ps[k][x], ds[k][x], sums[x], sums[x + 1])
        elif low + count - 1 <= x <= high - count + 1:
            sums[x] = [s + p for s, p in zip(sums[x], ps[k][x])]

    for t in range(low, high + 2 * count + 1):
        if t <= high:
            ps[0][t] = load_p(t)
            if low + count - 1 <= t <= high - count + 1:
                sums[t] = ps[0][t]
            if low < t < high:
                ds[0][t] = load_d(t)
        for k in range(1, count + 1):
            x = t - 2 * k
            if low + k <= x <= high - k:
                substep(k, x)


def own_divergence(u, west, v, inverse):
    lane = lanes(inverse.shape)
    first, last = lane == 0, lane == 127
    v = [v[0], v[1], jnp.where(last, 0.0, v[2])]
    up = [pltpu.roll(a, 1, 1) for a in v]
    south = [jnp.where(first, up[i - 1], up[i]) for i in range(3)]
    return [((a - w) + (b - s)) * inverse for a, w, b, s in zip(u, west, v, south)]


def winds(u, v, c, here, east):
    last = lanes(c.shape) == 127
    down = [pltpu.roll(s, 127, 1) for s in here]
    north = [jnp.where(last, down[1], down[0]), jnp.where(last, down[2], down[1]), down[2]]
    u = [a - c * (e - s) for a, e, s in zip(u, east, here)]
    v = [a - c * (n - s) for a, n, s in zip(v, north, here)]
    return u, [v[0], v[1], jnp.where(last, 0.0, v[2])]


def by_level(row):
    return jnp.broadcast_to(row, (128, row.shape[1])).T


def level_constants(courant_row, c_mem):
    c = by_level(courant_row)
    c_mem[0] = c
    c_mem[1] = c * c
    c_mem[2] = 1.0 / c


def group_rows(g):
    return pl.ds(8 * g, 8) if g < LEVELS // 8 else slice(LEVELS // 8 * 8, LEVELS)


def by_groups(work):
    def group(g, carry):
        work(pl.ds(pl.multiple_of(g * 8, 8), 8))
        return carry

    lax.fori_loop(0, LEVELS // 8, group, 0)
    work(group_rows(LEVELS // 8))


def silu(z):
    half = z * 0.5
    return half + half * jnp.tanh(half)


def normed_rows(read, gain, xs):
    columns = jnp.concatenate([jnp.concatenate(read(x), axis=0) for x in xs], axis=1)
    values = columns.astype(BF16).astype(F32)
    mean = jnp.sum(values * values, axis=0, keepdims=True) * (1.0 / ROWS)
    return (values * lax.rsqrt(mean + 1e-05) * gain).astype(BF16).T


def network(rows, w1, b1, w2, b2, w3, h1, h2, raw, beside=()):
    for n in range(0, UNITS, TILE):
        z = lax.dot_general(rows[...], w1[:, n : n + TILE], NN, preferred_element_type=F32)
        h1[:, n : n + TILE] = silu(z + b1[:, n : n + TILE]).astype(BF16)
    for n in range(0, UNITS, TILE):
        z = lax.dot_general(h1[...], w2[:, n : n + TILE], NN, preferred_element_type=F32)
        h2[:, n : n + TILE] = silu(z + b2[:, n : n + TILE]).astype(BF16)
        if n // TILE < len(beside):
            beside[n // TILE]()
    raw[...] = lax.dot_general(h2[...], w3[...], NN, preferred_element_type=F32)


def store_tendency(raw, mask, xs, places, out):
    t = raw[...].T.astype(BF16).astype(F32)
    for i, (x, place) in enumerate(zip(xs, places)):
        row = jnp.concatenate([mask[3 * x + j : 3 * x + j + 1, :] for j in range(3)], axis=1)
        listed = jnp.where(row > 0.5, t[:, i * ACROSS : (i + 1) * ACROSS], 0.0)
        for f in range(3):
            out[place, f] = listed[f * LEVELS : (f + 1) * LEVELS]


WEIGHTS_SCRATCH = [
    pltpu.VMEM((ROWS, UNITS), BF16),
    pltpu.VMEM((1, UNITS), F32),
    pltpu.VMEM((UNITS, UNITS), BF16),
    pltpu.VMEM((1, UNITS), F32),
    pltpu.VMEM((ROWS, UNITS), BF16),
    pltpu.VMEM((UNITS, ROWS), BF16),
    pltpu.VMEM((CHUNK, UNITS), BF16),
    pltpu.VMEM((CHUNK, UNITS), BF16),
    pltpu.VMEM((3, CHUNK, ROWS), BF16),
    pltpu.VMEM((3, CHUNK, ROWS), F32),
]


def network_flops(columns):
    return 2 * columns * (2 * ROWS * UNITS + UNITS * UNITS)


def interior_kernel(
    p_hbm, u_hbm, v_hbm, w1_hbm, b1_hbm, w2_hbm, b2_hbm, w3_hbm, courant, gain, lists,
    tend, mid, mask,
    p_mem, u_mem, v_mem, m_mem, t_mem, c_mem, one_x, one_y,
    w1, b1, w2, b2, w3t, w3, h1, h2, rows_mem, raw, sems,
):
    near, far = slice(0, 8), slice(8, WIDTH)
    fields = run_copies(
        [(f.at[s], m.at[s]) for s in (near, far)
         for f, m in ((p_hbm, p_mem), (u_hbm, u_mem), (v_hbm, v_mem))],
        sems,
    )
    weights = run_copies([(w3_hbm, w3t), (w1_hbm, w1), (b1_hbm, b1), (w2_hbm, w2), (b2_hbm, b2)],
                         sems, 6)
    level_constants(courant[...], c_mem)
    gain_column = by_level(gain[...])[:, :1]
    for s in range(SLOTS):
        entry = lists[s]
        part, spot = entry >> 7, entry & 127
        where = slice(s * DEVICES, (s + 1) * DEVICES)
        one_x[:, where] = (
            lax.broadcasted_iota(jnp.int32, (48, DEVICES), 0) == part
        ).astype(F32).astype(BF16)
        one_y[:, where] = (
            lax.broadcasted_iota(jnp.int32, (128, DEVICES), 0) == spot
        ).astype(F32).astype(BF16)
    mask[...] = lax.dot_general(one_x[...], one_y[...], NT, preferred_element_type=F32)

    def pair(i):
        def group(rows):
            c, square, inverse = (c_mem[j, rows, :] for j in range(3))

            def done(x, p, d, here, east):
                u, v = winds(split(u_mem[x, rows, :]), split(v_mem[x, rows, :]), c, here, east)
                for f, value in enumerate((p, u, v)):
                    m_mem[f, x - 3, rows, :] = join(value)

            def load_d(x):
                return own_divergence(split(u_mem[x, rows, :]), split(u_mem[x - 1, rows, :]),
                                      split(v_mem[x, rows, :]), inverse)

            march(3, 2 * i, 2 * i + 7, square, lambda x: split(p_mem[x, rows, :]), load_d, done)

        return group

    def read(x):
        return [m_mem[f, x] for f in range(3)]

    def prepare(i):
        rows_mem[i] = normed_rows(read, gain_column, (2 * i, 2 * i + 1))

    sent = []

    def post(i):
        xs = (2 * i, 2 * i + 1)
        store_tendency(raw.at[i], mask, [x + 3 for x in xs], xs, t_mem)
        sent.extend(run_copies([(t_mem.at[2 * i : 2 * i + 2], tend.at[2 * i : 2 * i + 2])],
                               sems, 11 + i))

    def some(i, low, high):
        def run():
            for g in range(low, high):
                pair(i)(group_rows(g))
        return run

    def both(*works):
        def run():
            for work in works:
                work()
        return run

    for copy in fields[:3]:
        copy.wait()
    by_groups(pair(0))
    for copy in fields[3:]:
        copy.wait()
    prepare(0)
    for copy in weights:
        copy.wait()
    w3[...] = w3t[...].T
    beside = (
        [some(1, 0, 3), some(1, 3, 6), both(some(1, 6, 8), some(2, 0, 1)),
         both(lambda: prepare(1), some(2, 1, 2))],
        [both(some(2, 2, 4), lambda: post(0)), some(2, 4, 6), some(2, 6, 8),
         lambda: prepare(2)],
        [lambda: sent.extend(run_copies([(m_mem, mid)], sems, 14)), lambda: post(1)],
    )
    for i in range(3):
        network(rows_mem.at[i], w1, b1, w2, b2, w3, h1, h2, raw.at[i], beside[i])
    post(2)
    for copy in sent:
        copy.wait()


def interior(p, u, v, weights, courant, gain, lists):
    column = pltpu.VMEM((WIDTH, LEVELS, ACROSS), F32)
    return pl.pallas_call(
        interior_kernel,
        out_shape=(
            jax.ShapeDtypeStruct((WIDTH // 2, 3, LEVELS, ACROSS), F32),
            jax.ShapeDtypeStruct((3, WIDTH // 2, LEVELS, ACROSS), F32),
            jax.ShapeDtypeStruct((48, 128), F32),
        ),
        in_specs=[ANY] * 8 + [VMEM] * 3,
        out_specs=(ANY, ANY, VMEM),
        scratch_shapes=[column] * 3
        + [pltpu.VMEM((3, WIDTH // 2, LEVELS, ACROSS), F32)]
        + [pltpu.VMEM((WIDTH // 2, 3, LEVELS, ACROSS), F32), pltpu.VMEM((3, LEVELS, 128), F32)]
        + [pltpu.VMEM((48, SLOTS * DEVICES), BF16), pltpu.VMEM((128, SLOTS * DEVICES), BF16)]
        + WEIGHTS_SCRATCH
        + [pltpu.SemaphoreType.DMA((15,))],
        compiler_params=pltpu.CompilerParams(vmem_limit_bytes=52 * 2**20),
        cost_estimate=pl.CostEstimate(
            flops=network_flops(WIDTH // 2 * ACROSS), bytes_accessed=8 * 2**20, transcendentals=0
        ),
        name="interior",
    )(p, u, v, *weights, courant, gain, lists)


def finish_kernel(
    p_hbm, u_hbm, v_hbm, left, right, tend, mid, w1_hbm, b1_hbm, w2_hbm, b2_hbm, w3_hbm,
    mask, courant, gain,
    p_out, u_out, v_out,
    p_mem, u_mem, v_mem, e_mem, halo, a_mem, b_mem, d_mem, g_mem, t_mem, c_mem,
    p_new, u_new, v_new,
    w1, b1, w2, b2, w3t, w3, h1, h2, rows_mem, raw, sems,
):
    near, far = slice(0, HALO), slice(HALO, WIDTH)
    fields = run_copies(
        [
            (left, halo.at[0]),
            (p_hbm.at[near], p_mem.at[HALO : 2 * HALO]),
            (u_hbm.at[near], u_mem.at[near]),
            (v_hbm.at[near], v_mem.at[near]),
            (right, halo.at[1]),
            (p_hbm.at[far], p_mem.at[2 * HALO : 3 * HALO]),
            (u_hbm.at[far], u_mem.at[far]),
            (v_hbm.at[far], v_mem.at[far]),
        ],
        sems,
    )
    weights = run_copies(
        [(w3_hbm, w3t), (w1_hbm, w1), (b1_hbm, b1), (w2_hbm, w2), (b2_hbm, b2),
         (mid.at[0], a_mem.at[6:12]), (mid.at[1], b_mem.at[3:9]), (mid.at[2], d_mem.at[3:9]),
         (tend, t_mem.at[3:9])],
        sems, 8,
    )
    level_constants(courant[...], c_mem)
    gain_column = by_level(gain[...])[:, :1]

    def loads(rows, inverse):
        def load_p(x):
            return split(p_mem[x + HALO, rows, :])

        def load_d(x):
            if x < 0:
                return [d * inverse for d in split(e_mem[x + HALO - 1, rows, :])]
            if x > WIDTH:
                return [d * inverse for d in split(e_mem[x - HALO, rows, :])]
            if x == WIDTH:
                return [(d - u) * inverse for d, u in zip(split(e_mem[HALO, rows, :]),
                                                          split(u_mem[WIDTH - 1, rows, :]))]
            west = u_mem[x - 1, rows, :] if x else e_mem[HALO - 1, rows, :]
            return own_divergence(split(u_mem[x, rows, :]), split(west),
                                  split(v_mem[x, rows, :]), inverse)

        return load_p, load_d

    def strip(low):
        def group(rows):
            c, square, inverse = (c_mem[i, rows, :] for i in range(3))

            def done(x, p, d, here, east):
                a_mem[x + 3, rows, :] = join(p)
                u, v = winds(split(u_mem[x, rows, :]), split(v_mem[x, rows, :]), c, here, east)
                b_mem[x, rows, :] = join(u)
                d_mem[x, rows, :] = join(v)
                if x == 0:
                    g_mem[3, rows, :] = join(d)

            march(3, low, low + 8, square, *loads(rows, inverse), done)

        by_groups(group)

    for copy in fields[:4]:
        copy.wait()
    for i in range(HALO):
        p_mem[i] = halo[0, i].astype(F32)
        e_mem[i] = halo[0, HALO + i].astype(F32)
    p_mem[HALO - 1] = p_mem[HALO - 1] + halo[0, 2 * HALO].astype(F32)
    p_mem[HALO - 2] = p_mem[HALO - 2] + halo[0, 2 * HALO + 1].astype(F32)
    e_mem[HALO - 2] = e_mem[HALO - 2] + halo[0, 2 * HALO + 2].astype(F32)
    e_mem[HALO - 1] = e_mem[HALO - 1] + halo[0, 2 * HALO + 3].astype(F32)
    strip(-3)
    for copy in fields[4:]:
        copy.wait()
    for i in range(HALO):
        p_mem[HALO + WIDTH + i] = halo[1, i].astype(F32)
        e_mem[HALO + i] = halo[1, HALO + i].astype(F32)
    for i in range(2):
        p_mem[HALO + WIDTH + i] = p_mem[HALO + WIDTH + i] + halo[1, 2 * HALO + i].astype(F32)
        e_mem[HALO + i] = e_mem[HALO + i] + halo[1, 2 * HALO + 2 + i].astype(F32)
    strip(6)

    def dynamics(g):
        rows = group_rows(g)
        c, square, inverse = (c_mem[i, rows, :] for i in range(3))

        def outer(x, p, d, here, east):
            a_mem[x + 3, rows, :] = join(p)
            g_mem[x + 3 if x < 0 else x - 8, rows, :] = join(d)

        march(3, -6, 2, square, *loads(rows, inverse), outer)
        march(3, 9, 17, square, *loads(rows, inverse), outer)

        def load_d(x):
            if 0 < x < WIDTH:
                return own_divergence(split(b_mem[x, rows, :]), split(b_mem[x - 1, rows, :]),
                                      split(d_mem[x, rows, :]), inverse)
            return split(g_mem[x + 3 if x <= 0 else x - 8, rows, :])

        def done(x, p, d, here, east):
            p_new[x, rows, :] = join(p)
            u, v = winds(split(b_mem[x, rows, :]), split(d_mem[x, rows, :]), c, here, east)
            u_new[x, rows, :] = join(u)
            v_new[x, rows, :] = join(v)

        march(3, -3, 14, square, lambda x: split(a_mem[x + 3, rows, :]), load_d, done)

    columns = (0, 1, 2, 9, 10, 11)

    def read(x):
        return a_mem[x + 3], b_mem[x], d_mem[x]

    def prepare(i):
        rows_mem[i] = normed_rows(read, gain_column, columns[2 * i : 2 * i + 2])

    def post(i):
        xs = columns[2 * i : 2 * i + 2]
        store_tendency(raw.at[i], mask, xs, xs, t_mem)

    outs = []

    def send(low, high):
        for x in range(low, high):
            for f, new in enumerate((p_new, u_new, v_new)):
                new[x] = new[x] + t_mem[x, f]
        outs.extend(run_copies(
            [(new.at[low:high], out.at[low:high])
             for new, out in ((p_new, p_out), (u_new, u_out), (v_new, v_out))],
            sems, len(outs),
        ))

    def both(*works):
        def run():
            for work in works:
                work()
        return run

    def group(g):
        return lambda: dynamics(g)

    prepare(0)
    for copy in weights:
        copy.wait()
    w3[...] = w3t[...].T
    beside = (
        [group(0), group(1), group(2), lambda: prepare(1)],
        [group(3), group(4), group(5), both(lambda: prepare(2), lambda: post(0))],
        [group(6), group(7), both(lambda: post(1), lambda: send(0, 4)), lambda: send(4, 10)],
    )
    for i in range(3):
        network(rows_mem.at[i], w1, b1, w2, b2, w3, h1, h2, raw.at[i], beside[i])
    post(2)
    send(10, 12)
    for copy in outs:
        copy.wait()


def finish(p, u, v, left, right, tend, mid, weights, mask, courant, gain):
    shape = jax.ShapeDtypeStruct((WIDTH, LEVELS, ACROSS), F32)
    column = pltpu.VMEM((WIDTH, LEVELS, ACROSS), F32)
    return pl.pallas_call(
        finish_kernel,
        out_shape=(shape,) * 3,
        in_specs=[ANY] * 3 + [OPEN] * 2 + [ANY] * 7 + [VMEM] * 3,
        out_specs=(ANY,) * 3,
        scratch_shapes=[pltpu.VMEM((SPAN, LEVELS, ACROSS), F32)] + [column] * 3
        + [pltpu.VMEM((2, SENT, LEVELS, ACROSS), BF16)]
        + [pltpu.VMEM((WIDTH + 6, LEVELS, ACROSS), F32), column, column]
        + [pltpu.VMEM((7, LEVELS, ACROSS), F32)]
        + [pltpu.VMEM((WIDTH, 3, LEVELS, ACROSS), F32), pltpu.VMEM((3, LEVELS, 128), F32)]
        + [column] * 3
        + WEIGHTS_SCRATCH
        + [pltpu.SemaphoreType.DMA((17,))],
        compiler_params=pltpu.CompilerParams(vmem_limit_bytes=52 * 2**20),
        cost_estimate=pl.CostEstimate(
            flops=network_flops(WIDTH // 2 * ACROSS), bytes_accessed=12 * 2**20, transcendentals=0
        ),
        name="finish",
    )(p, u, v, left, right, tend, mid, *weights, mask, courant, gain)


def body(
    pressure, wind_x, wind_y, courant, send_list,
    norm_gain, w_first, b_first, w_second, b_second, w_last,
):
    p, u, v = [jnp.transpose(f, (1, 0, 2)) for f in (pressure, wind_x, wind_y)]
    courant, gain = courant.reshape(1, LEVELS), norm_gain.reshape(1, ROWS)
    lists = jnp.transpose(send_list, (2, 0, 1))
    weights = (w_first, b_first.reshape(1, UNITS), w_second, b_second.reshape(1, UNITS), w_last.T)
    to_next, to_prev = edges(p, u, v)
    left = lax.ppermute(to_next, AXES, [(i, (i + 1) % DEVICES) for i in range(DEVICES)])
    right = lax.ppermute(to_prev, AXES, [(i, (i - 1) % DEVICES) for i in range(DEVICES)])
    tend, mid, mask = interior(p, u, v, weights, courant, gain, lists)
    outs = finish(p, u, v, left, right, tend, mid, weights, mask, courant, gain)
    return tuple(jnp.transpose(f, (1, 0, 2)) for f in outs)


def solution(mesh):
    split = P(None, AXES, None)
    in_specs = (split,) * 3 + (P(), P(AXES, None, None)) + (P(),) * 6
    return jax.shard_map(
        body, mesh=mesh, in_specs=in_specs, out_specs=(split,) * 3, check_vma=False
    )
```

time: 50 us -> 51.7 us (1.034)
  local copies, waits for them, and re-layouts: 0.98 us -> 5.95 us
  Pallas kernels: 39.6 us -> 35.7 us
    unnamed x4 -> x22, local copies, waits for them, and re-layouts: 0.98 us -> 3.86 us
    pallas_call x1, Pallas kernels: 3.08 us -> 1.43 us  [edges(): pl.pallas_call(edges_kernel, out_shape=(shape, shape), in_specs=[ANY] * 3...]
    pallas_call x1, Pallas kernels: 16.1 us -> 14.9 us  [interior(): pl.pallas_call(interior_kernel, out_shape=(jax.ShapeDtypeStruct((WIDTH //...]
    ppermute x0 -> x2, local copies, waits for them, and re-layouts: none -> 1.23 us  [the longest x1 1.06 us: body(): lax.ppermute(to_prev, AXES, [(i, (i - 1) % DEVICES) for i in range(DEVICE...]
    pallas_call x1, Pallas kernels: 20.4 us -> 19.4 us  [finish(): pl.pallas_call(finish_kernel, out_shape=(shape,) * 3, in_specs=[ANY] * 3...]
    pallas_call x0 -> x2, local copies, waits for them, and re-layouts: none -> 0.86 us  [edges(): pl.pallas_call(edges_kernel, out_shape=(shape, shape), in_specs=[ANY] * 3...]
  transfers between devices with their start and end apart: 2 -> 2, of which waited for: 0 -> 1; matrix products, arithmetic and copies ran while one was open for 0% -> 3% of each run, Pallas kernels for 32% -> 29%
where the time goes in v2:
time: 51.7 us; the launch traced here: 51.4 us
  Pallas kernels  35.7 us (69%)
  starting transfers between devices  8.53 us (16%)
  local copies, waits for them, and re-layouts  5.95 us (12%)
  between operations  1 us (2%)
    pallas_call x1, Pallas kernels, finish(): pl.pallas_call(finish_kernel, out_shape=(shape,) * 3, in_specs=[ANY] * 3...  19.4 us
    pallas_call x1, Pallas kernels, interior(): pl.pallas_call(interior_kernel, out_shape=(jax.ShapeDtypeStruct((WIDTH //...  14.9 us
    ppermute x1, starting transfers between devices, body(): lax.ppermute(to_prev, AXES, [(i, (i - 1) % DEVICES) for i in range(DEVICE...  8.27 us
    unnamed x22, local copies, waits for them, and re-layouts  3.86 us
    pallas_call x1, Pallas kernels, edges(): pl.pallas_call(edges_kernel, out_shape=(shape, shape), in_specs=[ANY] * 3...  1.43 us
    ppermute x1, local copies, waits for them, and re-layouts, body(): lax.ppermute(to_prev, AXES, [(i, (i - 1) % DEVICES) for i in range(DEVICE...  1.06 us
  transfers between devices with their start and end apart: 2, of which 1 were waited for; matrix products, arithmetic and copies ran while one was open for 3% of the time, Pallas kernels for 29%

profile of v2, /device:TPU:0, one launch (start us, length us, event | category | flops | bytes accessed | tf_op | source)
XLA Modules:
  0.0 51.4 jit_solution(4900959580574223223)
XLA Ops:
  0.6 0.0 copy-start
  0.6 1.3 %copy-done = f32[60,12,384]{2,0,1:T(8,128)S(1)} copy-done((f32[60,12,384]{2,0,1:T(8,128)S(1)}, f32[60,12,384]{2,0,1:T(8,128)}, u32[]{:S(2)}) %copy-start) | copy-done | bytes 1105944
  1.9 0.0 copy-start.2
  1.9 1.3 %copy-done.2 = f32[60,12,384]{2,0,1:T(8,128)S(1)} copy-done((f32[60,12,384]{2,0,1:T(8,128)S(1)}, f32[60,12,384]{2,0,1:T(8,128)}, u32[]{:S(2)}) %copy-start.2) | copy-done | bytes 1105944
  3.2 1.3 %copy-done.3 = f32[60,12,384]{2,0,1:T(8,128)S(1)} copy-done((f32[60,12,384]{2,0,1:T(8,128)S(1)}, f32[60,12,384]{2,0,1:T(8,128)}, u32[]{:S(2)}) %copy-start.3) | copy-done | bytes 1105944
  4.4 1.4 %edges.1 = (bf16[16,60,384]{2,1,0:T(8,128)(2,1)S(1)}, bf16[16,60,384]{2,1,0:T(8,128)(2,1)S(1)}) custom-call(f32[12,60,384]{2,1,0:T(8,128)S(1)} %bitcast.13, f32[12,60,384]{2,1,0:T(8,128)S(1)} %bitcast.17, f32[12,60,384]{2,1,0:T(8,128)S(1)} %bitcast.20), custom_call_target="tpu_custom_call" | custom-call | tf_op jit(solution)/shard_map/edges/pallas_call | solution.py:94
  5.9 0.0 copy-start.1
  5.9 0.0 copy-start.4
  5.9 0.0 copy-start.5
  5.9 0.0 copy-start.6
  5.9 0.0 copy-start.7
  5.9 0.0 copy-start.8
  6.0 0.0 copy-start.9
  6.0 0.0 copy-start.10
  6.0 0.4 copy.15
  6.4 8.3 %collective-permute-start.1 = (bf16[16,60,384]{2,0,1:T(8,128)(2,1)S(1)}, bf16[16,60,384]{2,0,1:T(8,128)(2,1)S(1)}, u32[]{:S(2)}, u32[]{:S(2)}) collective-permute-start(bf16[16,60,384]{2,0,1:T(8,128)(2,1)S(1)} %copy.15), channel_id=1, source_target_pairs={{0,127},{1,0},{2,1},{3,2},{4,3},{5,4},{6,5},{7,6},{8,7},{9,8},{10,... | collective-permute-start | bytes 2211848 | tf_op jit(solution)/shard_map/ppermute | solution.py:549
  14.7 0.4 copy.14
  15.1 0.3 collective-permute-start
  15.4 0.0 copy-done.1
  15.4 0.0 copy-done.4
  15.4 0.0 copy-done.5
  15.4 0.0 copy-done.6
  15.4 0.0 copy-done.7
  15.4 0.0 copy-done.8
  15.4 0.0 copy-done.9
  15.5 0.0 copy-done.10
  15.5 14.9 %interior.1 = (f32[6,3,60,384]{3,2,1,0:T(8,128)}, f32[3,6,60,384]{3,2,1,0:T(8,128)}, f32[48,128]{1,0:T(8,128)S(1)}) custom-call(f32[12,60,384]{2,1,0:T(8,128)S(1)} %bitcast.14, f32[12,60,384]{2,1,0:T(8,128)} %bitcast.15, f32[12,60,384]{2,1,0:T(8,128)} %bitcast.18, bf16[180,1024]{1,0:T(8,128)(2,1)S(1)} %copy-done.4, f32[1,1024]{1,0:T(1,128)S(1)} %bitcast.24, ...), custom_call_target="tpu_custom_call" | custom-call | flops 6530531328 | bytes 8388608 | tf_op jit(solution)/shard_map/interior/pallas_call | solution.py:332
  30.3 0.0 collective-permute-done.1
  30.3 1.1 %copy.17.right = bf16[16,60,384]{2,1,0:T(8,128)(2,1)} copy(bf16[16,60,384]{2,0,1:T(8,128)(2,1)S(1)} %collective-permute-done.1) | data formatting | bytes 1474560 | tf_op jit(solution)/shard_map/ppermute | solution.py:549
  31.4 0.3 collective-permute-done
  31.7 0.2 copy.16.left
  31.9 19.4 %finish.1 = (f32[12,60,384]{2,1,0:T(8,128)}, f32[12,60,384]{2,1,0:T(8,128)}, f32[12,60,384]{2,1,0:T(8,128)}) custom-call(f32[12,60,384]{2,1,0:T(8,128)} %bitcast.12, f32[12,60,384]{2,1,0:T(8,128)} %bitcast.16, f32[12,60,384]{2,1,0:T(8,128)} %bitcast.19, bf16[16,60,384]{2,1,0:T(8,128)(2,1)S(1)} %copy.16.left, bf16[16,60,384]{2,1,0:T(8,128)(2,1)} %copy.17.right, ...), custom_call_target="tpu_custom_call" | custom-call | flops 6530531328 | bytes 12582912 | tf_op jit(solution)/shard_map/finish/pallas_call | solution.py:518
  (1 shorter events, 0.0 us)
Async XLA Ops:
  0.6 1.3 %copy-start = (f32[60,12,384]{2,0,1:T(8,128)S(1)}, f32[60,12,384]{2,0,1:T(8,128)}, u32[]{:S(2)}) copy-start(f32[60,12,384]{2,0,1:T(8,128)} %param.11) | copy-start | bytes 3317764
  1.9 1.3 %copy-start.2 = (f32[60,12,384]{2,0,1:T(8,128)S(1)}, f32[60,12,384]{2,0,1:T(8,128)}, u32[]{:S(2)}) copy-start(f32[60,12,384]{2,0,1:T(8,128)} %param.12) | copy-start | bytes 3317764
  3.2 1.3 %copy-start.3 = (f32[60,12,384]{2,0,1:T(8,128)S(1)}, f32[60,12,384]{2,0,1:T(8,128)}, u32[]{:S(2)}) copy-start(f32[60,12,384]{2,0,1:T(8,128)} %param.13) | copy-start | bytes 3317764
  5.9 9.5 %copy-start.1 = (f32[60,12,384]{2,0,1:T(8,128)S(1)}, f32[60,12,384]{2,0,1:T(8,128)}, u32[]{:S(2)}) copy-start(f32[60,12,384]{2,0,1:T(8,128)} %param.11) | copy-start | bytes 3317764
  5.9 9.5 %copy-start.4 = (bf16[180,1024]{1,0:T(8,128)(2,1)S(1)}, bf16[180,1024]{1,0:T(8,128)(2,1)}, u32[]{:S(2)}) copy-start(bf16[180,1024]{1,0:T(8,128)(2,1)} %w1_hbm.3) | copy-start | bytes 1105924
  5.9 9.5 %copy-start.5 = (bf16[1024,180]{0,1:T(8,128)(2,1)S(1)}, bf16[1024,180]{0,1:T(8,128)(2,1)}, u32[]{:S(2)}) copy-start(bf16[1024,180]{0,1:T(8,128)(2,1)} %param.21) | copy-start | bytes 1105924
  5.9 9.5 %copy-start.6 = (s32[1,128,36]{1,0,2:T(1,128)S(1)}, s32[1,128,36]{1,0,2:T(1,128)}, u32[]{:S(2)}) copy-start(s32[1,128,36]{1,0,2:T(1,128)} %param.15) | copy-start | bytes 55300
  5.9 9.5 %copy-start.7 = (f32[1024]{0:T(1024)S(1)}, f32[1024]{0:T(1024)}, u32[]{:S(2)}) copy-start(f32[1024]{0:T(1024)} %param.18) | copy-start | bytes 12292
  5.9 9.5 %copy-start.8 = (f32[1024]{0:T(1024)S(1)}, f32[1024]{0:T(1024)}, u32[]{:S(2)}) copy-start(f32[1024]{0:T(1024)} %param.20) | copy-start | bytes 12292
  6.0 9.5 %copy-start.9 = (f32[180]{0:T(256)S(1)}, f32[180]{0:T(256)}, u32[]{:S(2)}) copy-start(f32[180]{0:T(256)} %param.16) | copy-start | bytes 2164
  6.0 9.5 %copy-start.10 = (f32[60]{0:T(128)S(1)}, f32[60]{0:T(128)}, u32[]{:S(2)}) copy-start(f32[60]{0:T(128)} %param.14) | copy-start | bytes 724
  6.4 23.9 %collective-permute-start.1 = (bf16[16,60,384]{2,0,1:T(8,128)(2,1)S(1)}, bf16[16,60,384]{2,0,1:T(8,128)(2,1)S(1)}, u32[]{:S(2)}, u32[]{:S(2)}) collective-permute-start(bf16[16,60,384]{2,0,1:T(8,128)(2,1)S(1)} %copy.15), channel_id=1, source_target_pairs={{0,127},{1,0},{2,1},{3,2},{4,3},{5,4},{6,5},{7,6},{8,7},{9,8},{10,... | collective-permute-start | bytes 2211848 | tf_op jit(solution)/shard_map/ppermute | solution.py:549
  15.1 16.6 %collective-permute-start = (bf16[16,60,384]{2,0,1:T(8,128)(2,1)S(1)}, bf16[16,60,384]{2,0,1:T(8,128)(2,1)S(1)}, u32[]{:S(2)}, u32[]{:S(2)}) collective-permute-start(bf16[16,60,384]{2,0,1:T(8,128)(2,1)S(1)} %copy.14), channel_id=1, source_target_pairs={{0,1},{1,2},{2,3},{3,4},{4,5},{5,6},{6,7},{7,8},{8,9},{9,10},{10,1... | collective-permute-start | bytes 2211848 | tf_op jit(solution)/shard_map/ppermute | solution.py:548

commit v3 on v2

--- a/solution.py
+++ b/solution.py
@@ -9,7 +9,7 @@
 LEVELS, WIDTH, ACROSS, UNITS, SLOTS, DEVICES = 60, 12, 384, 1024, 36, 128
 ROWS = 3 * LEVELS
 HALO = 6
-SENT = 2 * HALO + 4
+SENT = 3 * HALO
 OPEN = pl.BlockSpec(memory_space=pl.ANY)
 SPAN = WIDTH + 2 * HALO
 CHUNK = 2 * ACROSS
@@ -66,12 +66,12 @@
         x = WIDTH - HALO + 1 + i
         div = (u_mem[x] - u_mem[x - 1]) + divergence(v_mem[x])
         r_mem[HALO + i] = div.astype(BF16)
-        if x == WIDTH - 1:
-            r_mem[2 * HALO + 2] = rest(div)
+        if x >= WIDTH - 2:
+            r_mem[2 * HALO + 2 + WIDTH - x] = rest(div)
     r_mem[2 * HALO - 1] = u_mem[WIDTH - 1].astype(BF16)
-    r_mem[2 * HALO] = rest(p_mem[WIDTH - 1])
-    r_mem[2 * HALO + 1] = rest(p_mem[WIDTH - 2])
-    r_mem[2 * HALO + 3] = rest(u_mem[WIDTH - 1])
+    for i in range(3):
+        r_mem[2 * HALO + i] = rest(p_mem[WIDTH - 1 - i])
+    r_mem[SENT - 1] = rest(u_mem[WIDTH - 1])
     out_next = run_copies([(r_mem, to_next)], sems, 6)
     for copy in loads[3:]:
         copy.wait()
@@ -81,10 +81,10 @@
         west = u_mem[x - 1] if x else 0.0
         div = (u_mem[x] - west) + divergence(v_mem[x])
         l_mem[HALO + x] = div.astype(BF16)
-        if x < 2:
-            l_mem[2 * HALO + 2 + x] = rest(div)
-    l_mem[2 * HALO] = rest(p_mem[0])
-    l_mem[2 * HALO + 1] = rest(p_mem[1])
+        if x < 3:
+            l_mem[2 * HALO + 3 + x] = rest(div)
+    for i in range(3):
+        l_mem[2 * HALO + i] = rest(p_mem[i])
     for copy in out_next + run_copies([(l_mem, to_prev)], sems, 7):
         copy.wait()
 
@@ -99,12 +99,12 @@
         scratch_shapes=[pltpu.VMEM((WIDTH, LEVELS, ACROSS), F32)] * 3
         + [pltpu.VMEM((SENT, LEVELS, ACROSS), BF16)] * 2
         + [pltpu.SemaphoreType.DMA((8,))],
-        compiler_params=pltpu.CompilerParams(vmem_limit_bytes=24 * 2**20),
+        compiler_params=pltpu.CompilerParams(vmem_limit_bytes=60 * 2**20),
         name="edges",
     )(p, u, v)
 
 
-def march(count, low, high, square, load_p, load_d, done):
+def stepping(count, low, high, square, load_p, load_d, done):
     ps = [{} for _ in range(count + 1)]
     ds = [{} for _ in range(count + 1)]
     sums = {}
@@ -138,6 +138,17 @@
             x = t - 2 * k
             if low + k <= x <= high - k:
                 substep(k, x)
+        yield
+
+
+def march(*args):
+    for _ in stepping(*args):
+        pass
+
+
+def march_both(one, two):
+    for _ in zip(stepping(*one), stepping(*two), strict=True):
+        pass
 
 
 def own_divergence(u, west, v, inverse):
@@ -374,12 +385,15 @@
         ],
         sems,
     )
-    weights = run_copies(
-        [(w3_hbm, w3t), (w1_hbm, w1), (b1_hbm, b1), (w2_hbm, w2), (b2_hbm, b2),
-         (mid.at[0], a_mem.at[6:12]), (mid.at[1], b_mem.at[3:9]), (mid.at[2], d_mem.at[3:9]),
-         (tend, t_mem.at[3:9])],
-        sems, 8,
-    )
+
+    def start_weights():
+        return run_copies(
+            [(w3_hbm, w3t), (w1_hbm, w1), (b1_hbm, b1), (w2_hbm, w2), (b2_hbm, b2),
+             (mid.at[0], a_mem.at[6:12]), (mid.at[1], b_mem.at[3:9]), (mid.at[2], d_mem.at[3:9]),
+             (tend, t_mem.at[3:9])],
+            sems, 8,
+        )
+
     level_constants(courant[...], c_mem)
     gain_column = by_level(gain[...])[:, :1]
 
@@ -401,41 +415,38 @@
 
         return load_p, load_d
 
-    def strip(low):
-        def group(rows):
-            c, square, inverse = (c_mem[i, rows, :] for i in range(3))
-
-            def done(x, p, d, here, east):
-                a_mem[x + 3, rows, :] = join(p)
-                u, v = winds(split(u_mem[x, rows, :]), split(v_mem[x, rows, :]), c, here, east)
-                b_mem[x, rows, :] = join(u)
-                d_mem[x, rows, :] = join(v)
-                if x == 0:
-                    g_mem[3, rows, :] = join(d)
-
-            march(3, low, low + 8, square, *loads(rows, inverse), done)
-
-        by_groups(group)
+    def strips(rows):
+        c, square, inverse = (c_mem[i, rows, :] for i in range(3))
+
+        def done(x, p, d, here, east):
+            a_mem[x + 3, rows, :] = join(p)
+            u, v = winds(split(u_mem[x, rows, :]), split(v_mem[x, rows, :]), c, here, east)
+            b_mem[x, rows, :] = join(u)
+            d_mem[x, rows, :] = join(v)
+            if x == 0:
+                g_mem[3, rows, :] = join(d)
+
+        common = (square, *loads(rows, inverse), done)
+        march_both((3, -3, 5, *common), (3, 6, 14, *common))
 
     for copy in fields[:4]:
         copy.wait()
     for i in range(HALO):
         p_mem[i] = halo[0, i].astype(F32)
         e_mem[i] = halo[0, HALO + i].astype(F32)
-    p_mem[HALO - 1] = p_mem[HALO - 1] + halo[0, 2 * HALO].astype(F32)
-    p_mem[HALO - 2] = p_mem[HALO - 2] + halo[0, 2 * HALO + 1].astype(F32)
-    e_mem[HALO - 2] = e_mem[HALO - 2] + halo[0, 2 * HALO + 2].astype(F32)
-    e_mem[HALO - 1] = e_mem[HALO - 1] + halo[0, 2 * HALO + 3].astype(F32)
-    strip(-3)
+    for i, (near_p, near_e) in enumerate(((1, 2), (2, 3), (3, 1))):
+        p_mem[HALO - near_p] = p_mem[HALO - near_p] + halo[0, 2 * HALO + i].astype(F32)
+        e_mem[HALO - near_e] = e_mem[HALO - near_e] + halo[0, 2 * HALO + 3 + i].astype(F32)
     for copy in fields[4:]:
         copy.wait()
     for i in range(HALO):
         p_mem[HALO + WIDTH + i] = halo[1, i].astype(F32)
         e_mem[HALO + i] = halo[1, HALO + i].astype(F32)
-    for i in range(2):
+    for i in range(3):
         p_mem[HALO + WIDTH + i] = p_mem[HALO + WIDTH + i] + halo[1, 2 * HALO + i].astype(F32)
-        e_mem[HALO + i] = e_mem[HALO + i] + halo[1, 2 * HALO + 2 + i].astype(F32)
-    strip(6)
+        e_mem[HALO + i] = e_mem[HALO + i] + halo[1, 2 * HALO + 3 + i].astype(F32)
+    weights = start_weights()
+    by_groups(strips)
 
     def dynamics(g):
         rows = group_rows(g)
@@ -445,8 +456,8 @@
             a_mem[x + 3, rows, :] = join(p)
             g_mem[x + 3 if x < 0 else x - 8, rows, :] = join(d)
 
-        march(3, -6, 2, square, *loads(rows, inverse), outer)
-        march(3, 9, 17, square, *loads(rows, inverse), outer)
+        common = (square, *loads(rows, inverse), outer)
+        march_both((3, -6, 2, *common), (3, 9, 17, *common))
 
         def load_d(x):
             if 0 < x < WIDTH:
@@ -528,7 +539,7 @@
         + [column] * 3
         + WEIGHTS_SCRATCH
         + [pltpu.SemaphoreType.DMA((17,))],
-        compiler_params=pltpu.CompilerParams(vmem_limit_bytes=52 * 2**20),
+        compiler_params=pltpu.CompilerParams(vmem_limit_bytes=44 * 2**20),
         cost_estimate=pl.CostEstimate(
             flops=network_flops(WIDTH // 2 * ACROSS), bytes_accessed=12 * 2**20, transcendentals=0
         ),

time: 51.7 us -> 48.7 us (0.942)
  local copies, waits for them, and re-layouts: 5.95 us -> 2.99 us
    pallas_call x1, Pallas kernels: 1.43 us -> 3.33 us  [edges(): pl.pallas_call(edges_kernel, out_shape=(shape, shape), in_specs=[ANY] * 3...]
    pallas_call x1, Pallas kernels: 19.4 us -> 17.9 us  [finish(): pl.pallas_call(finish_kernel, out_shape=(shape,) * 3, in_specs=[ANY] * 3...]
    ppermute x2 -> x0, local copies, waits for them, and re-layouts: 1.23 us -> none  [the longest x1 1.06 us: body(): lax.ppermute(to_prev, AXES, [(i, (i - 1) % DEVICES) for i in range(DEVICE...]
    unnamed x22 -> x24, local copies, waits for them, and re-layouts: 3.86 us -> 2.99 us
    pallas_call x2 -> x0, local copies, waits for them, and re-layouts: 0.86 us -> none  [edges(): pl.pallas_call(edges_kernel, out_shape=(shape, shape), in_specs=[ANY] * 3...]
  transfers between devices with their start and end apart: 2 -> 2, of which waited for: 1 -> 0; matrix products, arithmetic and copies ran while one was open for 3% -> 0% of each run, Pallas kernels for 29% -> 31%
where the time goes in v3:
time: 48.7 us; the launch traced here: 48.5 us
  Pallas kernels  36.2 us (74%)
  starting transfers between devices  8.35 us (17%)
  local copies, waits for them, and re-layouts  2.99 us (6%)
  between operations  0.97 us (2%)
    pallas_call x1, Pallas kernels, finish(): pl.pallas_call(finish_kernel, out_shape=(shape,) * 3, in_specs=[ANY] * 3...  17.9 us
    pallas_call x1, Pallas kernels, interior(): pl.pallas_call(interior_kernel, out_shape=(jax.ShapeDtypeStruct((WIDTH //...  15 us
    ppermute x1, starting transfers between devices, body(): lax.ppermute(to_prev, AXES, [(i, (i - 1) % DEVICES) for i in range(DEVICE...  8.27 us
    pallas_call x1, Pallas kernels, edges(): pl.pallas_call(edges_kernel, out_shape=(shape, shape), in_specs=[ANY] * 3...  3.33 us
    unnamed x24, local copies, waits for them, and re-layouts  2.99 us
  transfers between devices with their start and end apart: 2, of which 0 were waited for; matrix products, arithmetic and copies ran while one was open for 0% of the time, Pallas kernels for 31%

profile of v3, /device:TPU:0, one launch (start us, length us, event | category | flops | bytes accessed | tf_op | source)
XLA Modules:
  0.0 48.5 jit_solution(5358892599573482927)
XLA Ops:
  0.6 0.0 copy-start
  0.6 0.0 copy-start.3
  0.7 0.0 copy-start.4
  0.7 0.0 copy-start.5
  0.7 0.0 copy-start.6
  0.7 0.0 copy-start.7
  0.7 0.0 copy-start.8
  0.7 0.0 copy-start.9
  0.7 3.3 %edges.1 = (bf16[18,60,384]{2,1,0:T(8,128)(2,1)}, bf16[18,60,384]{2,1,0:T(8,128)(2,1)}) custom-call(f32[12,60,384]{2,1,0:T(8,128)} %bitcast.12, f32[12,60,384]{2,1,0:T(8,128)} %bitcast.15, f32[12,60,384]{2,1,0:T(8,128)} %bitcast.18), custom_call_target="tpu_custom_call" | custom-call | tf_op jit(solution)/shard_map/edges/pallas_call | solution.py:94
  4.1 0.1 collective-permute-start
  4.1 8.3 %collective-permute-start.1 = (bf16[18,60,384]{2,1,0:T(8,128)(2,1)}, bf16[18,60,384]{2,1,0:T(8,128)(2,1)S(1)}, u32[]{:S(2)}, u32[]{:S(2)}) collective-permute-start(bf16[18,60,384]{2,1,0:T(8,128)(2,1)} %get-tuple-element.12), channel_id=1, source_target_pairs={{0,127},{1,0},{2,1},{3,2},{4,3},{5,4},{6,5},{7,6},{8,7},{9,8},{10,... | collective-permute-start | bytes 2488328 | tf_op jit(solution)/shard_map/ppermute | solution.py:560
  12.4 0.0 copy-done
  12.4 0.0 copy-done.3
  12.4 0.0 copy-done.4
  12.4 0.0 copy-done.5
  12.4 0.0 copy-done.6
  12.4 0.0 copy-done.7
  12.4 0.0 copy-done.8
  12.5 0.0 copy-done.9
  12.5 0.0 copy-start.1
  12.5 0.0 copy-start.2
  12.5 15.0 %interior.1 = (f32[6,3,60,384]{3,2,1,0:T(8,128)}, f32[3,6,60,384]{3,2,1,0:T(8,128)}, f32[48,128]{1,0:T(8,128)S(1)}) custom-call(f32[12,60,384]{2,1,0:T(8,128)S(1)} %bitcast.13, f32[12,60,384]{2,1,0:T(8,128)} %bitcast.16, f32[12,60,384]{2,1,0:T(8,128)} %bitcast.19, bf16[180,1024]{1,0:T(8,128)(2,1)S(1)} %copy-done.3, f32[1,1024]{1,0:T(1,128)S(1)} %bitcast.24, ...), custom_call_target="tpu_custom_call" | custom-call | flops 6530531328 | bytes 8388608 | tf_op jit(solution)/shard_map/interior/pallas_call | solution.py:343
  27.5 0.0 collective-permute-done.left
  27.5 0.0 collective-permute-done.1.right
  27.5 0.0 copy-done.1
  27.5 0.0 copy-done.2
  27.5 0.0 copy-start.10
  27.6 1.5 %copy-done.10 = f32[6,3,60,384]{3,2,1,0:T(8,128)S(1)} copy-done((f32[6,3,60,384]{3,2,1,0:T(8,128)S(1)}, f32[6,3,60,384]{3,2,1,0:T(8,128)}, u32[]{:S(2)}) %copy-start.10) | copy-done | bytes 1658904
  29.0 0.0 copy-start.11
  29.0 1.5 %copy-done.11 = f32[3,6,60,384]{3,2,1,0:T(8,128)S(1)} copy-done((f32[3,6,60,384]{3,2,1,0:T(8,128)S(1)}, f32[3,6,60,384]{3,2,1,0:T(8,128)}, u32[]{:S(2)}) %copy-start.11) | copy-done | bytes 1658904
  30.5 17.9 %finish.1 = (f32[12,60,384]{2,1,0:T(8,128)}, f32[12,60,384]{2,1,0:T(8,128)}, f32[12,60,384]{2,1,0:T(8,128)}) custom-call(f32[12,60,384]{2,1,0:T(8,128)S(1)} %bitcast.14, f32[12,60,384]{2,1,0:T(8,128)S(1)} %bitcast.17, f32[12,60,384]{2,1,0:T(8,128)S(1)} %bitcast.20, bf16[18,60,384]{2,1,0:T(8,128)(2,1)S(1)} %collective-permute-done.left, ...), custom_call_target="tpu_custom_call" | custom-call | flops 6530531328 | bytes 12582912 | tf_op jit(solution)/shard_map/finish/pallas_call | solution.py:529
Async XLA Ops:
  0.6 11.8 %copy-start = (f32[60,12,384]{2,0,1:T(8,128)S(1)}, f32[60,12,384]{2,0,1:T(8,128)}, u32[]{:S(2)}) copy-start(f32[60,12,384]{2,0,1:T(8,128)} %param.11) | copy-start | bytes 3317764
  0.6 11.8 %copy-start.3 = (bf16[180,1024]{1,0:T(8,128)(2,1)S(1)}, bf16[180,1024]{1,0:T(8,128)(2,1)}, u32[]{:S(2)}) copy-start(bf16[180,1024]{1,0:T(8,128)(2,1)} %w1_hbm.3) | copy-start | bytes 1105924
  0.7 11.8 %copy-start.4 = (bf16[1024,180]{0,1:T(8,128)(2,1)S(1)}, bf16[1024,180]{0,1:T(8,128)(2,1)}, u32[]{:S(2)}) copy-start(bf16[1024,180]{0,1:T(8,128)(2,1)} %param.21) | copy-start | bytes 1105924
  0.7 11.8 %copy-start.5 = (s32[1,128,36]{1,0,2:T(1,128)S(1)}, s32[1,128,36]{1,0,2:T(1,128)}, u32[]{:S(2)}) copy-start(s32[1,128,36]{1,0,2:T(1,128)} %param.15) | copy-start | bytes 55300
  0.7 11.8 %copy-start.6 = (f32[1024]{0:T(1024)S(1)}, f32[1024]{0:T(1024)}, u32[]{:S(2)}) copy-start(f32[1024]{0:T(1024)} %param.18) | copy-start | bytes 12292
  0.7 11.8 %copy-start.7 = (f32[1024]{0:T(1024)S(1)}, f32[1024]{0:T(1024)}, u32[]{:S(2)}) copy-start(f32[1024]{0:T(1024)} %param.20) | copy-start | bytes 12292
  0.7 11.8 %copy-start.8 = (f32[180]{0:T(256)S(1)}, f32[180]{0:T(256)}, u32[]{:S(2)}) copy-start(f32[180]{0:T(256)} %param.16) | copy-start | bytes 2164
  0.7 11.8 %copy-start.9 = (f32[60]{0:T(128)S(1)}, f32[60]{0:T(128)}, u32[]{:S(2)}) copy-start(f32[60]{0:T(128)} %param.14) | copy-start | bytes 724
  4.1 23.5 %collective-permute-start = (bf16[18,60,384]{2,1,0:T(8,128)(2,1)}, bf16[18,60,384]{2,1,0:T(8,128)(2,1)S(1)}, u32[]{:S(2)}, u32[]{:S(2)}) collective-permute-start(bf16[18,60,384]{2,1,0:T(8,128)(2,1)} %get-tuple-element.11), channel_id=1, source_target_pairs={{0,1},{1,2},{2,3},{3,4},{4,5},{5,6},{6,7},{7,8},{8,9},{9,10},{10,1... | collective-permute-start | bytes 2488328 | tf_op jit(solution)/shard_map/ppermute | solution.py:559
  4.1 23.4 %collective-permute-start.1 = (bf16[18,60,384]{2,1,0:T(8,128)(2,1)}, bf16[18,60,384]{2,1,0:T(8,128)(2,1)S(1)}, u32[]{:S(2)}, u32[]{:S(2)}) collective-permute-start(bf16[18,60,384]{2,1,0:T(8,128)(2,1)} %get-tuple-element.12), channel_id=1, source_target_pairs={{0,127},{1,0},{2,1},{3,2},{4,3},{5,4},{6,5},{7,6},{8,7},{9,8},{10,... | collective-permute-start | bytes 2488328 | tf_op jit(solution)/shard_map/ppermute | solution.py:560
  12.5 15.1 %copy-start.1 = (f32[60,12,384]{2,0,1:T(8,128)S(1)}, f32[60,12,384]{2,0,1:T(8,128)}, u32[]{:S(2)}) copy-start(f32[60,12,384]{2,0,1:T(8,128)} %param.12) | copy-start | bytes 3317764
  12.5 15.1 %copy-start.2 = (f32[60,12,384]{2,0,1:T(8,128)S(1)}, f32[60,12,384]{2,0,1:T(8,128)}, u32[]{:S(2)}) copy-start(f32[60,12,384]{2,0,1:T(8,128)} %param.13) | copy-start | bytes 3317764
  27.5 1.5 %copy-start.10 = (f32[6,3,60,384]{3,2,1,0:T(8,128)S(1)}, f32[6,3,60,384]{3,2,1,0:T(8,128)}, u32[]{:S(2)}) copy-start(f32[6,3,60,384]{3,2,1,0:T(8,128)} %get-tuple-element.13.tend) | copy-start | bytes 4976644
  29.0 1.5 %copy-start.11 = (f32[3,6,60,384]{3,2,1,0:T(8,128)S(1)}, f32[3,6,60,384]{3,2,1,0:T(8,128)}, u32[]{:S(2)}) copy-start(f32[3,6,60,384]{3,2,1,0:T(8,128)} %get-tuple-element.14.mid) | copy-start | bytes 4976644

commit v4 on v3

--- a/solution.py
+++ b/solution.py
@@ -51,7 +51,7 @@
     return (value - value.astype(BF16).astype(F32)).astype(BF16)
 
 
-def edges_kernel(p_hbm, u_hbm, v_hbm, to_next, to_prev, p_mem, u_mem, v_mem, r_mem, l_mem, sems):
+def edges_kernel(p_hbm, u_hbm, v_hbm, r_mem, l_mem, p_mem, u_mem, v_mem, sems):
     low, high = slice(0, HALO), slice(WIDTH - HALO, WIDTH)
     loads = run_copies(
         [(f.at[s], m.at[s]) for s in (high, low)
@@ -72,7 +72,6 @@
     for i in range(3):
         r_mem[2 * HALO + i] = rest(p_mem[WIDTH - 1 - i])
     r_mem[SENT - 1] = rest(u_mem[WIDTH - 1])
-    out_next = run_copies([(r_mem, to_next)], sems, 6)
     for copy in loads[3:]:
         copy.wait()
     for i in range(HALO):
@@ -85,8 +84,6 @@
             l_mem[2 * HALO + 3 + x] = rest(div)
     for i in range(3):
         l_mem[2 * HALO + i] = rest(p_mem[i])
-    for copy in out_next + run_copies([(l_mem, to_prev)], sems, 7):
-        copy.wait()
 
 
 def edges(p, u, v):
@@ -95,10 +92,9 @@
         edges_kernel,
         out_shape=(shape, shape),
         in_specs=[ANY] * 3,
-        out_specs=(OPEN, OPEN),
+        out_specs=(VMEM, VMEM),
         scratch_shapes=[pltpu.VMEM((WIDTH, LEVELS, ACROSS), F32)] * 3
-        + [pltpu.VMEM((SENT, LEVELS, ACROSS), BF16)] * 2
-        + [pltpu.SemaphoreType.DMA((8,))],
+        + [pltpu.SemaphoreType.DMA((6,))],
         compiler_params=pltpu.CompilerParams(vmem_limit_bytes=60 * 2**20),
         name="edges",
     )(p, u, v)
@@ -272,22 +268,34 @@
         ).astype(F32).astype(BF16)
     mask[...] = lax.dot_general(one_x[...], one_y[...], NT, preferred_element_type=F32)
 
-    def pair(i):
-        def group(rows):
-            c, square, inverse = (c_mem[j, rows, :] for j in range(3))
-
-            def done(x, p, d, here, east):
-                u, v = winds(split(u_mem[x, rows, :]), split(v_mem[x, rows, :]), c, here, east)
-                for f, value in enumerate((p, u, v)):
-                    m_mem[f, x - 3, rows, :] = join(value)
-
-            def load_d(x):
-                return own_divergence(split(u_mem[x, rows, :]), split(u_mem[x - 1, rows, :]),
-                                      split(v_mem[x, rows, :]), inverse)
-
-            march(3, 2 * i, 2 * i + 7, square, lambda x: split(p_mem[x, rows, :]), load_d, done)
-
-        return group
+    def columns(rows, *pairs):
+        c, square, inverse = (c_mem[j, rows, :] for j in range(3))
+
+        def done(x, p, d, here, east):
+            u, v = winds(split(u_mem[x, rows, :]), split(v_mem[x, rows, :]), c, here, east)
+            for f, value in enumerate((p, u, v)):
+                m_mem[f, x - 3, rows, :] = join(value)
+
+        def load_d(x):
+            return own_divergence(split(u_mem[x, rows, :]), split(u_mem[x - 1, rows, :]),
+                                  split(v_mem[x, rows, :]), inverse)
+
+        return [(3, 2 * i, 2 * i + 7, square, lambda x: split(p_mem[x, rows, :]), load_d, done)
+                for i in pairs]
+
+    def first_pair(rows, more):
+        march_both(*columns(rows, 0), *columns(more, 0))
+
+    def two_groups(g, carry):
+        at = pl.multiple_of(g * 16, 16)
+        first_pair(pl.ds(at, 8), pl.ds(pl.multiple_of(at + 8, 8), 8))
+        return carry
+
+    def other_pairs(low, high):
+        def run():
+            for g in range(low, high):
+                march_both(*columns(group_rows(g), 1, 2))
+        return run
 
     def read(x):
         return [m_mem[f, x] for f in range(3)]
@@ -303,12 +311,6 @@
         sent.extend(run_copies([(t_mem.at[2 * i : 2 * i + 2], tend.at[2 * i : 2 * i + 2])],
                                sems, 11 + i))
 
-    def some(i, low, high):
-        def run():
-            for g in range(low, high):
-                pair(i)(group_rows(g))
-        return run
-
     def both(*works):
         def run():
             for work in works:
@@ -317,7 +319,8 @@
 
     for copy in fields[:3]:
         copy.wait()
-    by_groups(pair(0))
+    lax.fori_loop(0, LEVELS // 16, two_groups, 0)
+    first_pair(group_rows(6), group_rows(7))
     for copy in fields[3:]:
         copy.wait()
     prepare(0)
@@ -325,10 +328,9 @@
         copy.wait()
     w3[...] = w3t[...].T
     beside = (
-        [some(1, 0, 3), some(1, 3, 6), both(some(1, 6, 8), some(2, 0, 1)),
-         both(lambda: prepare(1), some(2, 1, 2))],
-        [both(some(2, 2, 4), lambda: post(0)), some(2, 4, 6), some(2, 6, 8),
-         lambda: prepare(2)],
+        [other_pairs(0, 2), other_pairs(2, 4), other_pairs(4, 6),
+         both(other_pairs(6, 8), lambda: prepare(1))],
+        [lambda: post(0), lambda: prepare(2)],
         [lambda: sent.extend(run_copies([(m_mem, mid)], sems, 14)), lambda: post(1)],
     )
     for i in range(3):
@@ -539,7 +541,7 @@
         + [column] * 3
         + WEIGHTS_SCRATCH
         + [pltpu.SemaphoreType.DMA((17,))],
-        compiler_params=pltpu.CompilerParams(vmem_limit_bytes=44 * 2**20),
+        compiler_params=pltpu.CompilerParams(vmem_limit_bytes=48 * 2**20),
         cost_estimate=pl.CostEstimate(
             flops=network_flops(WIDTH // 2 * ACROSS), bytes_accessed=12 * 2**20, transcendentals=0
         ),

time: 48.7 us -> 44 us (0.903)
  local copies, waits for them, and re-layouts: 2.99 us -> 0.05 us
  Pallas kernels: 36.2 us -> 34.5 us
    unnamed x24 -> x20, local copies, waits for them, and re-layouts: 2.99 us -> 0.05 us
    pallas_call x1, Pallas kernels: 15 us -> 14 us  [interior(): pl.pallas_call(interior_kernel, out_shape=(jax.ShapeDtypeStruct((WIDTH //...]
    pallas_call x1, Pallas kernels: 17.9 us -> 17.2 us  [finish(): pl.pallas_call(finish_kernel, out_shape=(shape,) * 3, in_specs=[ANY] * 3...]
  transfers between devices with their start and end apart: 2 -> 2, of which waited for: 0 -> 0; matrix products, arithmetic and copies ran while one was open for 0% -> 0% of each run, Pallas kernels for 31% -> 32%
where the time goes in v4:
time: 44 us; the launch traced here: 43.9 us
  Pallas kernels  34.5 us (78%)
  starting transfers between devices  8.35 us (19%)
  between operations  0.96 us (2%)
    pallas_call x1, Pallas kernels, finish(): pl.pallas_call(finish_kernel, out_shape=(shape,) * 3, in_specs=[ANY] * 3...  17.2 us
    pallas_call x1, Pallas kernels, interior(): pl.pallas_call(interior_kernel, out_shape=(jax.ShapeDtypeStruct((WIDTH //...  14 us
    ppermute x1, starting transfers between devices, body(): lax.ppermute(to_prev, AXES, [(i, (i - 1) % DEVICES) for i in range(DEVICE...  8.27 us
    pallas_call x1, Pallas kernels, edges(): pl.pallas_call(edges_kernel, out_shape=(shape, shape), in_specs=[ANY] * 3...  3.33 us
  transfers between devices with their start and end apart: 2, of which 0 were waited for; matrix products, arithmetic and copies ran while one was open for 0% of the time, Pallas kernels for 32%

profile of v4, /device:TPU:0, one launch (start us, length us, event | category | flops | bytes accessed | tf_op | source)
XLA Modules:
  0.0 43.9 jit_solution(13407325096310048793)
XLA Ops:
  0.6 0.0 copy-start
  0.6 0.0 copy-start.3
  0.7 0.0 copy-start.4
  0.7 0.0 copy-start.5
  0.7 0.0 copy-start.6
  0.7 0.0 copy-start.7
  0.7 0.0 copy-start.8
  0.7 0.0 copy-start.9
  0.7 3.3 %edges.1 = (bf16[18,60,384]{2,1,0:T(8,128)(2,1)}, bf16[18,60,384]{2,1,0:T(8,128)(2,1)}) custom-call(f32[12,60,384]{2,1,0:T(8,128)} %bitcast.12, f32[12,60,384]{2,1,0:T(8,128)} %bitcast.15, f32[12,60,384]{2,1,0:T(8,128)} %bitcast.18), custom_call_target="tpu_custom_call" | custom-call | tf_op jit(solution)/shard_map/edges/pallas_call | solution.py:91
  4.1 0.1 collective-permute-start
  4.1 8.3 %collective-permute-start.1 = (bf16[18,60,384]{2,1,0:T(8,128)(2,1)}, bf16[18,60,384]{2,1,0:T(8,128)(2,1)S(1)}, u32[]{:S(2)}, u32[]{:S(2)}) collective-permute-start(bf16[18,60,384]{2,1,0:T(8,128)(2,1)} %get-tuple-element.12), channel_id=1, source_target_pairs={{0,127},{1,0},{2,1},{3,2},{4,3},{5,4},{6,5},{7,6},{8,7},{9,8},{10,... | collective-permute-start | bytes 2488328 | tf_op jit(solution)/shard_map/ppermute | solution.py:562
  12.4 0.0 copy-done
  12.4 0.0 copy-done.3
  12.4 0.0 copy-done.4
  12.4 0.0 copy-done.5
  12.4 0.0 copy-done.6
  12.4 0.0 copy-done.7
  12.4 0.0 copy-done.8
  12.5 0.0 copy-done.9
  12.5 0.0 copy-start.1
  12.5 0.0 copy-start.2
  12.5 14.0 %interior.1 = (f32[6,3,60,384]{3,2,1,0:T(8,128)}, f32[3,6,60,384]{3,2,1,0:T(8,128)}, f32[48,128]{1,0:T(8,128)S(1)}) custom-call(f32[12,60,384]{2,1,0:T(8,128)S(1)} %bitcast.13, f32[12,60,384]{2,1,0:T(8,128)} %bitcast.16, f32[12,60,384]{2,1,0:T(8,128)} %bitcast.19, bf16[180,1024]{1,0:T(8,128)(2,1)S(1)} %copy-done.3, f32[1,1024]{1,0:T(1,128)S(1)} %bitcast.24, ...), custom_call_target="tpu_custom_call" | custom-call | flops 6530531328 | bytes 8388608 | tf_op jit(solution)/shard_map/interior/pallas_call | solution.py:345
  26.5 0.0 collective-permute-done.left
  26.5 0.0 collective-permute-done.1.right
  26.5 0.0 copy-done.1
  26.5 0.0 copy-done.2
  26.6 17.2 %finish.1 = (f32[12,60,384]{2,1,0:T(8,128)}, f32[12,60,384]{2,1,0:T(8,128)}, f32[12,60,384]{2,1,0:T(8,128)}) custom-call(f32[12,60,384]{2,1,0:T(8,128)S(1)} %bitcast.14, f32[12,60,384]{2,1,0:T(8,128)S(1)} %bitcast.17, f32[12,60,384]{2,1,0:T(8,128)S(1)} %bitcast.20, bf16[18,60,384]{2,1,0:T(8,128)(2,1)S(1)} %collective-permute-done.left, ...), custom_call_target="tpu_custom_call" | custom-call | flops 6530531328 | bytes 12582912 | tf_op jit(solution)/shard_map/finish/pallas_call | solution.py:531
Async XLA Ops:
  0.6 11.8 %copy-start = (f32[60,12,384]{2,0,1:T(8,128)S(1)}, f32[60,12,384]{2,0,1:T(8,128)}, u32[]{:S(2)}) copy-start(f32[60,12,384]{2,0,1:T(8,128)} %param.11) | copy-start | bytes 3317764
  0.6 11.8 %copy-start.3 = (bf16[180,1024]{1,0:T(8,128)(2,1)S(1)}, bf16[180,1024]{1,0:T(8,128)(2,1)}, u32[]{:S(2)}) copy-start(bf16[180,1024]{1,0:T(8,128)(2,1)} %w1_hbm.3) | copy-start | bytes 1105924
  0.7 11.8 %copy-start.4 = (bf16[1024,180]{0,1:T(8,128)(2,1)S(1)}, bf16[1024,180]{0,1:T(8,128)(2,1)}, u32[]{:S(2)}) copy-start(bf16[1024,180]{0,1:T(8,128)(2,1)} %param.21) | copy-start | bytes 1105924
  0.7 11.8 %copy-start.5 = (s32[1,128,36]{1,0,2:T(1,128)S(1)}, s32[1,128,36]{1,0,2:T(1,128)}, u32[]{:S(2)}) copy-start(s32[1,128,36]{1,0,2:T(1,128)} %param.15) | copy-start | bytes 55300
  0.7 11.8 %copy-start.6 = (f32[1024]{0:T(1024)S(1)}, f32[1024]{0:T(1024)}, u32[]{:S(2)}) copy-start(f32[1024]{0:T(1024)} %param.18) | copy-start | bytes 12292
  0.7 11.8 %copy-start.7 = (f32[1024]{0:T(1024)S(1)}, f32[1024]{0:T(1024)}, u32[]{:S(2)}) copy-start(f32[1024]{0:T(1024)} %param.20) | copy-start | bytes 12292
  0.7 11.8 %copy-start.8 = (f32[180]{0:T(256)S(1)}, f32[180]{0:T(256)}, u32[]{:S(2)}) copy-start(f32[180]{0:T(256)} %param.16) | copy-start | bytes 2164
  0.7 11.8 %copy-start.9 = (f32[60]{0:T(128)S(1)}, f32[60]{0:T(128)}, u32[]{:S(2)}) copy-start(f32[60]{0:T(128)} %param.14) | copy-start | bytes 724
  4.1 22.5 %collective-permute-start = (bf16[18,60,384]{2,1,0:T(8,128)(2,1)}, bf16[18,60,384]{2,1,0:T(8,128)(2,1)S(1)}, u32[]{:S(2)}, u32[]{:S(2)}) collective-permute-start(bf16[18,60,384]{2,1,0:T(8,128)(2,1)} %get-tuple-element.11), channel_id=1, source_target_pairs={{0,1},{1,2},{2,3},{3,4},{4,5},{5,6},{6,7},{7,8},{8,9},{9,10},{10,1... | collective-permute-start | bytes 2488328 | tf_op jit(solution)/shard_map/ppermute | solution.py:561
  4.1 22.4 %collective-permute-start.1 = (bf16[18,60,384]{2,1,0:T(8,128)(2,1)}, bf16[18,60,384]{2,1,0:T(8,128)(2,1)S(1)}, u32[]{:S(2)}, u32[]{:S(2)}) collective-permute-start(bf16[18,60,384]{2,1,0:T(8,128)(2,1)} %get-tuple-element.12), channel_id=1, source_target_pairs={{0,127},{1,0},{2,1},{3,2},{4,3},{5,4},{6,5},{7,6},{8,7},{9,8},{10,... | collective-permute-start | bytes 2488328 | tf_op jit(solution)/shard_map/ppermute | solution.py:562
  12.5 14.1 %copy-start.1 = (f32[60,12,384]{2,0,1:T(8,128)S(1)}, f32[60,12,384]{2,0,1:T(8,128)}, u32[]{:S(2)}) copy-start(f32[60,12,384]{2,0,1:T(8,128)} %param.12) | copy-start | bytes 3317764
  12.5 14.1 %copy-start.2 = (f32[60,12,384]{2,0,1:T(8,128)S(1)}, f32[60,12,384]{2,0,1:T(8,128)}, u32[]{:S(2)}) copy-start(f32[60,12,384]{2,0,1:T(8,128)} %param.13) | copy-start | bytes 3317764

commit v5 on v4

--- a/solution.py
+++ b/solution.py
@@ -10,8 +10,6 @@
 ROWS = 3 * LEVELS
 HALO = 6
 SENT = 3 * HALO
-OPEN = pl.BlockSpec(memory_space=pl.ANY)
-SPAN = WIDTH + 2 * HALO
 CHUNK = 2 * ACROSS
 TILE = 256
 F32, BF16 = jnp.float32, jnp.bfloat16
@@ -366,42 +364,27 @@
 
 
 def finish_kernel(
-    p_hbm, u_hbm, v_hbm, left, right, tend, mid, w1_hbm, b1_hbm, w2_hbm, b2_hbm, w3_hbm,
+    p_own, u_mem, v_mem, left, right, tend, mid, w1_hbm, b1_hbm, w2_hbm, b2_hbm, w3_hbm,
     mask, courant, gain,
     p_out, u_out, v_out,
-    p_mem, u_mem, v_mem, e_mem, halo, a_mem, b_mem, d_mem, g_mem, t_mem, c_mem,
+    p_mem, e_mem, a_mem, b_mem, d_mem, g_mem, t_mem, c_mem,
     p_new, u_new, v_new,
     w1, b1, w2, b2, w3t, w3, h1, h2, rows_mem, raw, sems,
 ):
-    near, far = slice(0, HALO), slice(HALO, WIDTH)
-    fields = run_copies(
-        [
-            (left, halo.at[0]),
-            (p_hbm.at[near], p_mem.at[HALO : 2 * HALO]),
-            (u_hbm.at[near], u_mem.at[near]),
-            (v_hbm.at[near], v_mem.at[near]),
-            (right, halo.at[1]),
-            (p_hbm.at[far], p_mem.at[2 * HALO : 3 * HALO]),
-            (u_hbm.at[far], u_mem.at[far]),
-            (v_hbm.at[far], v_mem.at[far]),
-        ],
-        sems,
+    weights = run_copies(
+        [(w3_hbm, w3t), (w1_hbm, w1), (b1_hbm, b1), (w2_hbm, w2), (b2_hbm, b2),
+         (mid.at[0], a_mem.at[6:12]), (mid.at[1], b_mem.at[3:9]), (mid.at[2], d_mem.at[3:9]),
+         (tend, t_mem.at[3:9])],
+        sems, 8,
     )
-
-    def start_weights():
-        return run_copies(
-            [(w3_hbm, w3t), (w1_hbm, w1), (b1_hbm, b1), (w2_hbm, w2), (b2_hbm, b2),
-             (mid.at[0], a_mem.at[6:12]), (mid.at[1], b_mem.at[3:9]), (mid.at[2], d_mem.at[3:9]),
-             (tend, t_mem.at[3:9])],
-            sems, 8,
-        )
-
     level_constants(courant[...], c_mem)
     gain_column = by_level(gain[...])[:, :1]
 
     def loads(rows, inverse):
         def load_p(x):
-            return split(p_mem[x + HALO, rows, :])
+            if 0 <= x < WIDTH:
+                return split(p_own[x, rows, :])
+            return split(p_mem[x + HALO if x < 0 else x - HALO, rows, :])
 
         def load_d(x):
             if x < 0:
@@ -431,23 +414,16 @@
         common = (square, *loads(rows, inverse), done)
         march_both((3, -3, 5, *common), (3, 6, 14, *common))
 
-    for copy in fields[:4]:
-        copy.wait()
     for i in range(HALO):
-        p_mem[i] = halo[0, i].astype(F32)
-        e_mem[i] = halo[0, HALO + i].astype(F32)
+        p_mem[i] = left[i].astype(F32)
+        e_mem[i] = left[HALO + i].astype(F32)
+        p_mem[HALO + i] = right[i].astype(F32)
+        e_mem[HALO + i] = right[HALO + i].astype(F32)
     for i, (near_p, near_e) in enumerate(((1, 2), (2, 3), (3, 1))):
-        p_mem[HALO - near_p] = p_mem[HALO - near_p] + halo[0, 2 * HALO + i].astype(F32)
-        e_mem[HALO - near_e] = e_mem[HALO - near_e] + halo[0, 2 * HALO + 3 + i].astype(F32)
-    for copy in fields[4:]:
-        copy.wait()
-    for i in range(HALO):
-        p_mem[HALO + WIDTH + i] = halo[1, i].astype(F32)
-        e_mem[HALO + i] = halo[1, HALO + i].astype(F32)
-    for i in range(3):
-        p_mem[HALO + WIDTH + i] = p_mem[HALO + WIDTH + i] + halo[1, 2 * HALO + i].astype(F32)
-        e_mem[HALO + i] = e_mem[HALO + i] + halo[1, 2 * HALO + 3 + i].astype(F32)
-    weights = start_weights()
+        p_mem[HALO - near_p] = p_mem[HALO - near_p] + left[2 * HALO + i].astype(F32)
+        e_mem[HALO - near_e] = e_mem[HALO - near_e] + left[2 * HALO + 3 + i].astype(F32)
+        p_mem[HALO + i] = p_mem[HALO + i] + right[2 * HALO + i].astype(F32)
+        e_mem[HALO + i] = e_mem[HALO + i] + right[2 * HALO + 3 + i].astype(F32)
     by_groups(strips)
 
     def dynamics(g):
@@ -531,10 +507,9 @@
     return pl.pallas_call(
         finish_kernel,
         out_shape=(shape,) * 3,
-        in_specs=[ANY] * 3 + [OPEN] * 2 + [ANY] * 7 + [VMEM] * 3,
+        in_specs=[VMEM] * 5 + [ANY] * 7 + [VMEM] * 3,
         out_specs=(ANY,) * 3,
-        scratch_shapes=[pltpu.VMEM((SPAN, LEVELS, ACROSS), F32)] + [column] * 3
-        + [pltpu.VMEM((2, SENT, LEVELS, ACROSS), BF16)]
+        scratch_shapes=[column] * 2
         + [pltpu.VMEM((WIDTH + 6, LEVELS, ACROSS), F32), column, column]
         + [pltpu.VMEM((7, LEVELS, ACROSS), F32)]
         + [pltpu.VMEM((WIDTH, 3, LEVELS, ACROSS), F32), pltpu.VMEM((3, LEVELS, 128), F32)]

time: 44 us -> 42.8 us (0.973)
  Pallas kernels: 34.5 us -> 33.4 us
    pallas_call x1, Pallas kernels: 17.2 us -> 16 us  [finish(): pl.pallas_call(finish_kernel, out_shape=(shape,) * 3, in_specs=[VMEM] * 5...]
  transfers between devices with their start and end apart: 2 -> 2, of which waited for: 0 -> 0; matrix products, arithmetic and copies ran while one was open for 0% -> 0% of each run, Pallas kernels for 32% -> 33%
where the time goes in v5:
time: 42.8 us; the launch traced here: 42.7 us
  Pallas kernels  33.4 us (78%)
  starting transfers between devices  8.35 us (20%)
  between operations  0.96 us (2%)
    pallas_call x1, Pallas kernels, finish(): pl.pallas_call(finish_kernel, out_shape=(shape,) * 3, in_specs=[VMEM] * 5...  16 us
    pallas_call x1, Pallas kernels, interior(): pl.pallas_call(interior_kernel, out_shape=(jax.ShapeDtypeStruct((WIDTH //...  14 us
    ppermute x1, starting transfers between devices, body(): lax.ppermute(to_prev, AXES, [(i, (i - 1) % DEVICES) for i in range(DEVICE...  8.27 us
    pallas_call x1, Pallas kernels, edges(): pl.pallas_call(edges_kernel, out_shape=(shape, shape), in_specs=[ANY] * 3...  3.33 us
  transfers between devices with their start and end apart: 2, of which 0 were waited for; matrix products, arithmetic and copies ran while one was open for 0% of the time, Pallas kernels for 33%

profile of v5, /device:TPU:0, one launch (start us, length us, event | category | flops | bytes accessed | tf_op | source)
XLA Modules:
  0.0 42.7 jit_solution(13623241547475768471)
XLA Ops:
  0.6 0.0 copy-start
  0.6 0.0 copy-start.3
  0.7 0.0 copy-start.4
  0.7 0.0 copy-start.5
  0.7 0.0 copy-start.6
  0.7 0.0 copy-start.7
  0.7 0.0 copy-start.8
  0.7 0.0 copy-start.9
  0.7 3.3 %edges.1 = (bf16[18,60,384]{2,1,0:T(8,128)(2,1)}, bf16[18,60,384]{2,1,0:T(8,128)(2,1)}) custom-call(f32[12,60,384]{2,1,0:T(8,128)} %bitcast.12, f32[12,60,384]{2,1,0:T(8,128)} %bitcast.15, f32[12,60,384]{2,1,0:T(8,128)} %bitcast.18), custom_call_target="tpu_custom_call" | custom-call | tf_op jit(solution)/shard_map/edges/pallas_call | solution.py:89
  4.1 0.1 collective-permute-start
  4.1 8.3 %collective-permute-start.1 = (bf16[18,60,384]{2,1,0:T(8,128)(2,1)}, bf16[18,60,384]{2,1,0:T(8,128)(2,1)S(1)}, u32[]{:S(2)}, u32[]{:S(2)}) collective-permute-start(bf16[18,60,384]{2,1,0:T(8,128)(2,1)} %get-tuple-element.12), channel_id=1, source_target_pairs={{0,127},{1,0},{2,1},{3,2},{4,3},{5,4},{6,5},{7,6},{8,7},{9,8},{10,... | collective-permute-start | bytes 2488328 | tf_op jit(solution)/shard_map/ppermute | solution.py:537
  12.4 0.0 copy-done
  12.4 0.0 copy-done.3
  12.4 0.0 copy-done.4
  12.4 0.0 copy-done.5
  12.4 0.0 copy-done.6
  12.4 0.0 copy-done.7
  12.4 0.0 copy-done.8
  12.5 0.0 copy-done.9
  12.5 0.0 copy-start.1
  12.5 0.0 copy-start.2
  12.5 14.0 %interior.1 = (f32[6,3,60,384]{3,2,1,0:T(8,128)}, f32[3,6,60,384]{3,2,1,0:T(8,128)}, f32[48,128]{1,0:T(8,128)S(1)}) custom-call(f32[12,60,384]{2,1,0:T(8,128)S(1)} %bitcast.13, f32[12,60,384]{2,1,0:T(8,128)} %bitcast.16, f32[12,60,384]{2,1,0:T(8,128)} %bitcast.19, bf16[180,1024]{1,0:T(8,128)(2,1)S(1)} %copy-done.3, f32[1,1024]{1,0:T(1,128)S(1)} %bitcast.24, ...), custom_call_target="tpu_custom_call" | custom-call | flops 6530531328 | bytes 8388608 | tf_op jit(solution)/shard_map/interior/pallas_call | solution.py:343
  26.5 0.0 collective-permute-done.left
  26.5 0.0 collective-permute-done.1.right
  26.5 0.0 copy-done.1
  26.5 0.0 copy-done.2
  26.6 16.0 %finish.1 = (f32[12,60,384]{2,1,0:T(8,128)}, f32[12,60,384]{2,1,0:T(8,128)}, f32[12,60,384]{2,1,0:T(8,128)}) custom-call(f32[12,60,384]{2,1,0:T(8,128)S(1)} %bitcast.14, f32[12,60,384]{2,1,0:T(8,128)S(1)} %bitcast.17, f32[12,60,384]{2,1,0:T(8,128)S(1)} %bitcast.20, bf16[18,60,384]{2,1,0:T(8,128)(2,1)S(1)} %collective-permute-done.left, ...), custom_call_target="tpu_custom_call" | custom-call | flops 6530531328 | bytes 12582912 | tf_op jit(solution)/shard_map/finish/pallas_call | solution.py:507
Async XLA Ops:
  0.6 11.8 %copy-start = (f32[60,12,384]{2,0,1:T(8,128)S(1)}, f32[60,12,384]{2,0,1:T(8,128)}, u32[]{:S(2)}) copy-start(f32[60,12,384]{2,0,1:T(8,128)} %param.11) | copy-start | bytes 3317764
  0.6 11.8 %copy-start.3 = (bf16[180,1024]{1,0:T(8,128)(2,1)S(1)}, bf16[180,1024]{1,0:T(8,128)(2,1)}, u32[]{:S(2)}) copy-start(bf16[180,1024]{1,0:T(8,128)(2,1)} %w1_hbm.3) | copy-start | bytes 1105924
  0.7 11.8 %copy-start.4 = (bf16[1024,180]{0,1:T(8,128)(2,1)S(1)}, bf16[1024,180]{0,1:T(8,128)(2,1)}, u32[]{:S(2)}) copy-start(bf16[1024,180]{0,1:T(8,128)(2,1)} %param.21) | copy-start | bytes 1105924
  0.7 11.8 %copy-start.5 = (s32[1,128,36]{1,0,2:T(1,128)S(1)}, s32[1,128,36]{1,0,2:T(1,128)}, u32[]{:S(2)}) copy-start(s32[1,128,36]{1,0,2:T(1,128)} %param.15) | copy-start | bytes 55300
  0.7 11.8 %copy-start.6 = (f32[1024]{0:T(1024)S(1)}, f32[1024]{0:T(1024)}, u32[]{:S(2)}) copy-start(f32[1024]{0:T(1024)} %param.18) | copy-start | bytes 12292
  0.7 11.8 %copy-start.7 = (f32[1024]{0:T(1024)S(1)}, f32[1024]{0:T(1024)}, u32[]{:S(2)}) copy-start(f32[1024]{0:T(1024)} %param.20) | copy-start | bytes 12292
  0.7 11.8 %copy-start.8 = (f32[180]{0:T(256)S(1)}, f32[180]{0:T(256)}, u32[]{:S(2)}) copy-start(f32[180]{0:T(256)} %param.16) | copy-start | bytes 2164
  0.7 11.8 %copy-start.9 = (f32[60]{0:T(128)S(1)}, f32[60]{0:T(128)}, u32[]{:S(2)}) copy-start(f32[60]{0:T(128)} %param.14) | copy-start | bytes 724
  4.1 22.5 %collective-permute-start = (bf16[18,60,384]{2,1,0:T(8,128)(2,1)}, bf16[18,60,384]{2,1,0:T(8,128)(2,1)S(1)}, u32[]{:S(2)}, u32[]{:S(2)}) collective-permute-start(bf16[18,60,384]{2,1,0:T(8,128)(2,1)} %get-tuple-element.11), channel_id=1, source_target_pairs={{0,1},{1,2},{2,3},{3,4},{4,5},{5,6},{6,7},{7,8},{8,9},{9,10},{10,1... | collective-permute-start | bytes 2488328 | tf_op jit(solution)/shard_map/ppermute | solution.py:536
  4.1 22.4 %collective-permute-start.1 = (bf16[18,60,384]{2,1,0:T(8,128)(2,1)}, bf16[18,60,384]{2,1,0:T(8,128)(2,1)S(1)}, u32[]{:S(2)}, u32[]{:S(2)}) collective-permute-start(bf16[18,60,384]{2,1,0:T(8,128)(2,1)} %get-tuple-element.12), channel_id=1, source_target_pairs={{0,127},{1,0},{2,1},{3,2},{4,3},{5,4},{6,5},{7,6},{8,7},{9,8},{10,... | collective-permute-start | bytes 2488328 | tf_op jit(solution)/shard_map/ppermute | solution.py:537
  12.5 14.1 %copy-start.1 = (f32[60,12,384]{2,0,1:T(8,128)S(1)}, f32[60,12,384]{2,0,1:T(8,128)}, u32[]{:S(2)}) copy-start(f32[60,12,384]{2,0,1:T(8,128)} %param.12) | copy-start | bytes 3317764
  12.5 14.1 %copy-start.2 = (f32[60,12,384]{2,0,1:T(8,128)S(1)}, f32[60,12,384]{2,0,1:T(8,128)}, u32[]{:S(2)}) copy-start(f32[60,12,384]{2,0,1:T(8,128)} %param.13) | copy-start | bytes 3317764

commit v6 on v5

--- a/solution.py
+++ b/solution.py
@@ -56,10 +56,13 @@
          for f, m in ((p_hbm, p_mem), (u_hbm, u_mem), (v_hbm, v_mem))],
         sems,
     )
-    for copy in loads[:3]:
-        copy.wait()
+    loads[0].wait()
     for i in range(HALO):
         r_mem[i] = p_mem[WIDTH - HALO + i].astype(BF16)
+    for i in range(3):
+        r_mem[2 * HALO + i] = rest(p_mem[WIDTH - 1 - i])
+    for copy in loads[1:3]:
+        copy.wait()
     for i in range(HALO - 1):
         x = WIDTH - HALO + 1 + i
         div = (u_mem[x] - u_mem[x - 1]) + divergence(v_mem[x])
@@ -67,8 +70,6 @@
         if x >= WIDTH - 2:
             r_mem[2 * HALO + 2 + WIDTH - x] = rest(div)
     r_mem[2 * HALO - 1] = u_mem[WIDTH - 1].astype(BF16)
-    for i in range(3):
-        r_mem[2 * HALO + i] = rest(p_mem[WIDTH - 1 - i])
     r_mem[SENT - 1] = rest(u_mem[WIDTH - 1])
     for copy in loads[3:]:
         copy.wait()

time: 42.8 us -> 42.8 us (level)
  no operation moved by 1% of the time
where the time goes in v6:
time: 42.8 us; the launch traced here: 42.7 us
  Pallas kernels  33.4 us (78%)
  starting transfers between devices  8.35 us (20%)
  between operations  0.96 us (2%)
    pallas_call x1, Pallas kernels, finish(): pl.pallas_call(finish_kernel, out_shape=(shape,) * 3, in_specs=[VMEM] * 5...  16 us
    pallas_call x1, Pallas kernels, interior(): pl.pallas_call(interior_kernel, out_shape=(jax.ShapeDtypeStruct((WIDTH //...  14 us
    ppermute x1, starting transfers between devices, body(): lax.ppermute(to_prev, AXES, [(i, (i - 1) % DEVICES) for i in range(DEVICE...  8.27 us
    pallas_call x1, Pallas kernels, edges(): pl.pallas_call(edges_kernel, out_shape=(shape, shape), in_specs=[ANY] * 3...  3.33 us
  transfers between devices with their start and end apart: 2, of which 0 were waited for; matrix products, arithmetic and copies ran while one was open for 0% of the time, Pallas kernels for 33%

profile of v6, /device:TPU:0, one launch (start us, length us, event | category | flops | bytes accessed | tf_op | source)
XLA Modules:
  0.0 42.7 jit_solution(9183768899200907022)
XLA Ops:
  0.6 0.0 copy-start
  0.6 0.0 copy-start.3
  0.7 0.0 copy-start.4
  0.7 0.0 copy-start.5
  0.7 0.0 copy-start.6
  0.7 0.0 copy-start.7
  0.7 0.0 copy-start.8
  0.7 0.0 copy-start.9
  0.7 3.3 %edges.1 = (bf16[18,60,384]{2,1,0:T(8,128)(2,1)}, bf16[18,60,384]{2,1,0:T(8,128)(2,1)}) custom-call(f32[12,60,384]{2,1,0:T(8,128)} %bitcast.12, f32[12,60,384]{2,1,0:T(8,128)} %bitcast.15, f32[12,60,384]{2,1,0:T(8,128)} %bitcast.18), custom_call_target="tpu_custom_call" | custom-call | tf_op jit(solution)/shard_map/edges/pallas_call | solution.py:90
  4.1 0.1 collective-permute-start
  4.1 8.3 %collective-permute-start.1 = (bf16[18,60,384]{2,1,0:T(8,128)(2,1)}, bf16[18,60,384]{2,1,0:T(8,128)(2,1)S(1)}, u32[]{:S(2)}, u32[]{:S(2)}) collective-permute-start(bf16[18,60,384]{2,1,0:T(8,128)(2,1)} %get-tuple-element.12), channel_id=1, source_target_pairs={{0,127},{1,0},{2,1},{3,2},{4,3},{5,4},{6,5},{7,6},{8,7},{9,8},{10,... | collective-permute-start | bytes 2488328 | tf_op jit(solution)/shard_map/ppermute | solution.py:538
  12.4 0.0 copy-done
  12.4 0.0 copy-done.3
  12.4 0.0 copy-done.4
  12.4 0.0 copy-done.5
  12.4 0.0 copy-done.6
  12.4 0.0 copy-done.7
  12.4 0.0 copy-done.8
  12.5 0.0 copy-done.9
  12.5 0.0 copy-start.1
  12.5 0.0 copy-start.2
  12.5 14.0 %interior.1 = (f32[6,3,60,384]{3,2,1,0:T(8,128)}, f32[3,6,60,384]{3,2,1,0:T(8,128)}, f32[48,128]{1,0:T(8,128)S(1)}) custom-call(f32[12,60,384]{2,1,0:T(8,128)S(1)} %bitcast.13, f32[12,60,384]{2,1,0:T(8,128)} %bitcast.16, f32[12,60,384]{2,1,0:T(8,128)} %bitcast.19, bf16[180,1024]{1,0:T(8,128)(2,1)S(1)} %copy-done.3, f32[1,1024]{1,0:T(1,128)S(1)} %bitcast.24, ...), custom_call_target="tpu_custom_call" | custom-call | flops 6530531328 | bytes 8388608 | tf_op jit(solution)/shard_map/interior/pallas_call | solution.py:344
  26.5 0.0 collective-permute-done.left
  26.5 0.0 collective-permute-done.1.right
  26.5 0.0 copy-done.1
  26.5 0.0 copy-done.2
  26.6 16.0 %finish.1 = (f32[12,60,384]{2,1,0:T(8,128)}, f32[12,60,384]{2,1,0:T(8,128)}, f32[12,60,384]{2,1,0:T(8,128)}) custom-call(f32[12,60,384]{2,1,0:T(8,128)S(1)} %bitcast.14, f32[12,60,384]{2,1,0:T(8,128)S(1)} %bitcast.17, f32[12,60,384]{2,1,0:T(8,128)S(1)} %bitcast.20, bf16[18,60,384]{2,1,0:T(8,128)(2,1)S(1)} %collective-permute-done.left, ...), custom_call_target="tpu_custom_call" | custom-call | flops 6530531328 | bytes 12582912 | tf_op jit(solution)/shard_map/finish/pallas_call | solution.py:508
Async XLA Ops:
  0.6 11.8 %copy-start = (f32[60,12,384]{2,0,1:T(8,128)S(1)}, f32[60,12,384]{2,0,1:T(8,128)}, u32[]{:S(2)}) copy-start(f32[60,12,384]{2,0,1:T(8,128)} %param.11) | copy-start | bytes 3317764
  0.6 11.8 %copy-start.3 = (bf16[180,1024]{1,0:T(8,128)(2,1)S(1)}, bf16[180,1024]{1,0:T(8,128)(2,1)}, u32[]{:S(2)}) copy-start(bf16[180,1024]{1,0:T(8,128)(2,1)} %w1_hbm.3) | copy-start | bytes 1105924
  0.7 11.8 %copy-start.4 = (bf16[1024,180]{0,1:T(8,128)(2,1)S(1)}, bf16[1024,180]{0,1:T(8,128)(2,1)}, u32[]{:S(2)}) copy-start(bf16[1024,180]{0,1:T(8,128)(2,1)} %param.21) | copy-start | bytes 1105924
  0.7 11.8 %copy-start.5 = (s32[1,128,36]{1,0,2:T(1,128)S(1)}, s32[1,128,36]{1,0,2:T(1,128)}, u32[]{:S(2)}) copy-start(s32[1,128,36]{1,0,2:T(1,128)} %param.15) | copy-start | bytes 55300
  0.7 11.8 %copy-start.6 = (f32[1024]{0:T(1024)S(1)}, f32[1024]{0:T(1024)}, u32[]{:S(2)}) copy-start(f32[1024]{0:T(1024)} %param.18) | copy-start | bytes 12292
  0.7 11.8 %copy-start.7 = (f32[1024]{0:T(1024)S(1)}, f32[1024]{0:T(1024)}, u32[]{:S(2)}) copy-start(f32[1024]{0:T(1024)} %param.20) | copy-start | bytes 12292
  0.7 11.8 %copy-start.8 = (f32[180]{0:T(256)S(1)}, f32[180]{0:T(256)}, u32[]{:S(2)}) copy-start(f32[180]{0:T(256)} %param.16) | copy-start | bytes 2164
  0.7 11.8 %copy-start.9 = (f32[60]{0:T(128)S(1)}, f32[60]{0:T(128)}, u32[]{:S(2)}) copy-start(f32[60]{0:T(128)} %param.14) | copy-start | bytes 724
  4.1 22.5 %collective-permute-start = (bf16[18,60,384]{2,1,0:T(8,128)(2,1)}, bf16[18,60,384]{2,1,0:T(8,128)(2,1)S(1)}, u32[]{:S(2)}, u32[]{:S(2)}) collective-permute-start(bf16[18,60,384]{2,1,0:T(8,128)(2,1)} %get-tuple-element.11), channel_id=1, source_target_pairs={{0,1},{1,2},{2,3},{3,4},{4,5},{5,6},{6,7},{7,8},{8,9},{9,10},{10,1... | collective-permute-start | bytes 2488328 | tf_op jit(solution)/shard_map/ppermute | solution.py:537
  4.1 22.4 %collective-permute-start.1 = (bf16[18,60,384]{2,1,0:T(8,128)(2,1)}, bf16[18,60,384]{2,1,0:T(8,128)(2,1)S(1)}, u32[]{:S(2)}, u32[]{:S(2)}) collective-permute-start(bf16[18,60,384]{2,1,0:T(8,128)(2,1)} %get-tuple-element.12), channel_id=1, source_target_pairs={{0,127},{1,0},{2,1},{3,2},{4,3},{5,4},{6,5},{7,6},{8,7},{9,8},{10,... | collective-permute-start | bytes 2488328 | tf_op jit(solution)/shard_map/ppermute | solution.py:538
  12.5 14.1 %copy-start.1 = (f32[60,12,384]{2,0,1:T(8,128)S(1)}, f32[60,12,384]{2,0,1:T(8,128)}, u32[]{:S(2)}) copy-start(f32[60,12,384]{2,0,1:T(8,128)} %param.12) | copy-start | bytes 3317764
  12.5 14.1 %copy-start.2 = (f32[60,12,384]{2,0,1:T(8,128)S(1)}, f32[60,12,384]{2,0,1:T(8,128)}, u32[]{:S(2)}) copy-start(f32[60,12,384]{2,0,1:T(8,128)} %param.13) | copy-start | bytes 3317764
